TPU v7x, 512 devices: a whole 4x4x16 slice. The times are simulated.
512 devices in a mesh: seq: 64 (over x, z_lo, core), dp: 8 (over z_hi, y).
Axes of the slice: x: 4, y: 4, z: 16 (z_hi: 2, z_lo: 8; z = z_hi * 8 + z_lo), core: 2. Of those that a mesh axis runs over, the one named last changes fastest.
Arguments:
- bases: int32 [8, 32768], P('dp', 'seq'), may hold values from 0 to 3
- w_embed: bfloat16 [60, 768], replicated, may hold values from -1.5 to 1.5
- b_embed: float32 [768], replicated, may hold values from -3 to 3
- gain: float32 [768], replicated, may hold values from 0.25 to 1.75
- taps: float32 [3, 768], replicated, may hold values from -3.5 to 3.5
- w_widen: bfloat16 [768, 896], replicated, may hold values from -0.21875 to 0.21875
- cotangent: bfloat16 [8, 16384, 896], P('dp', 'seq'), may hold values from -0.109375 to 0.109375
Outputs:
- grad_embed: float32 [60, 768], replicated
- grad_bias: float32 [768], replicated
- grad_gain: float32 [768], replicated
- grad_taps: float32 [3, 768], replicated
- grad_widen: float32 [768, 896], P('dp', 'seq')
All inputs are finite; a program needn't handle non-finite values.
Results may differ from a plain program's by a relative error of at most 0.007.
Values may be sent and summed in bfloat16 or wider, within the bound.
A program may use at most 128 MiB of HBM per device.

v0:
```python
import jax
import jax.numpy as jnp
from jax import lax
from jax.sharding import PartitionSpec as P

KE = 15
DILATION_STEP = 64


def padded(block, sides, width):
    for axis, dim in sides:
        count = lax.axis_size(axis)
        forward = [(i, i + 1) for i in range(count - 1)]
        backward = [(target, source) for source, target in forward]
        low = lax.ppermute(
            lax.slice_in_dim(block, block.shape[dim] - width, None, axis=dim), axis, forward
        )
        high = lax.ppermute(lax.slice_in_dim(block, 0, width, axis=dim), axis, backward)
        block = jnp.concatenate([low, block, high], axis=dim)
    return block


def make_patches(extended, length):
    window = jnp.stack([extended[j : j + length] for j in range(KE)], axis=1)
    table = window[:, :, None] == jnp.arange(1, 5, dtype=jnp.int32)[None, None, :]
    return table.reshape(length, KE * 4).astype(jnp.bfloat16)


def norm_gelu(value_entries, gain):
    meansq = jnp.mean(value_entries * value_entries, axis=-1, keepdims=True)
    return jax.nn.gelu(value_entries * lax.rsqrt(meansq + 1e-06) * gain)


def dilated(padded_input, kernel_rows, element_count):
    grand_total = kernel_rows[1] * padded_input[
        DILATION_STEP : DILATION_STEP + element_count
    ].astype(jnp.float32)
    grand_total = grand_total + kernel_rows[0] * padded_input[0:element_count].astype(jnp.float32)
    return grand_total + kernel_rows[2] * padded_input[
        2 * DILATION_STEP : 2 * DILATION_STEP + element_count
    ].astype(jnp.float32)


def transposed(padded_input, kernel_rows, element_count):
    grand_total = kernel_rows[1] * padded_input[
        DILATION_STEP : DILATION_STEP + element_count
    ].astype(jnp.float32)
    grand_total = grand_total + kernel_rows[0] * padded_input[
        2 * DILATION_STEP : 2 * DILATION_STEP + element_count
    ].astype(jnp.float32)
    return grand_total + kernel_rows[2] * padded_input[0:element_count].astype(jnp.float32)


def tap_sums(grad, padded_input, element_count):
    float_gradient = grad.astype(jnp.float32)
    return jnp.stack(
        [
            jnp.sum(
                float_gradient
                * padded_input[
                    kernel_position * DILATION_STEP : kernel_position * DILATION_STEP
                    + element_count
                ].astype(jnp.float32),
                axis=0,
            )
            for kernel_position in range(3)
        ]
    )


def with_rims(value_entries):
    return padded(value_entries, (("seq", 0),), DILATION_STEP)


def local(bases, w_embed, b_embed, gain, taps, w_widen, cotangent):
    length = bases.shape[1]
    element_count = length // 2
    width = w_embed.shape[1]
    extended = padded(bases + 1, (("seq", 1),), KE // 2)[0]
    patches = make_patches(extended, length)
    embedded = jnp.dot(patches, w_embed, preferred_element_type=jnp.float32) + b_embed
    pooled = (jnp.sum(embedded.reshape(element_count, 2, width), axis=1) * 0.5).astype(jnp.bfloat16)
    act_f, pull = jax.vjp(norm_gelu, pooled.astype(jnp.float32), gain)
    activation_rows = act_f.astype(jnp.bfloat16)
    cot = cotangent[0]
    block_gradient = lax.dot_general(
        cot, w_widen, (((1,), (1,)), ((), ())), preferred_element_type=jnp.float32
    ).astype(jnp.bfloat16)
    activation_padded = with_rims(activation_rows)
    mixed = dilated(activation_padded, taps, element_count)
    padded_gradient = with_rims(block_gradient)
    g_taps = tap_sums(block_gradient, activation_padded, element_count)
    d_act = transposed(padded_gradient, taps, element_count)
    block = (pooled.astype(jnp.float32) + mixed).astype(jnp.bfloat16)
    mine = lax.psum_scatter(
        lax.dot_general(cot, block, (((0,), (0,)), ((), ())), preferred_element_type=jnp.float32),
        "seq",
        scatter_dimension=0,
        tiled=True,
    )
    g_widen = lax.psum_scatter(mine, "dp", scatter_dimension=1, tiled=True).T
    d_norm, g_gain = pull(d_act)
    half = ((block_gradient.astype(jnp.float32) + d_norm) * 0.5).astype(jnp.bfloat16)
    paired = jnp.sum(patches.reshape(element_count, 2, KE * 4), axis=1)
    g_embed = lax.dot_general(
        paired, half, (((0,), (0,)), ((), ())), preferred_element_type=jnp.float32
    )
    g_bias = 2.0 * jnp.sum(half.astype(jnp.float32), axis=0)
    totals = lax.psum((g_embed, g_bias, g_gain, g_taps), ("seq", "dp"))
    return (totals[0], totals[1], totals[2], totals[3], g_widen)


def solution(mesh):
    return jax.shard_map(
        local,
        mesh=mesh,
        in_specs=(P("dp", "seq"), P(), P(), P(), P(), P(), P("dp", "seq", None)),
        out_specs=(P(), P(), P(), P(), P("dp", "seq")),
        check_vma=False,
    )
```

profile of v0, /device:TPU:1, one launch (start us, length us, event | category | flops | bytes accessed | tf_op | source)
XLA Modules:
  0.0 1372.7 jit_solution(12467370611043151436)
XLA Ops:
  8.0 0.0 copy-start
  8.0 0.0 all-reduce.7.cloned.1.call-start
  8.1 0.8 fusion.39
  8.9 0.1 fusion.44
  8.9 4.9 collective-permute-start
  13.9 0.0 copy-start.2
  13.9 0.0 copy-start.5
  13.9 5.3 collective-permute-start.1
  19.2 1.6 convolution_convert_fusion
  20.8 0.7 fusion.43
  21.5 1.9 collective-permute-start.3
  23.4 3.0 collective-permute-start.2
  26.4 0.1 eq.34
  26.6 0.1 fusion.36
  26.7 0.1 add_bitcast_fusion
  26.7 0.1 fusion.35
  26.8 0.1 stack.75
  27.0 1.6 convolution_add_fusion
  28.7 2.2 reshape.79
  30.9 0.0 copy-start.3
  30.9 2.9 reduce_sum.93
  33.8 1.3 fusion.23
  35.2 2.0 fusion.10
  37.2 0.0 copy-start.1
  37.2 0.9 convert_reduce_fusion
  38.1 2.6 collective-permute-start.4
  40.7 1.9 collective-permute-start.5
  42.6 4.0 collective-permute-done.5
  46.6 2.3 convolution_bitcast_fusion
  48.9 0.0 all-reduce.7.cloned.1.call-update
  48.9 0.0 reduce-scatter.3.cloned.1.call-start
  49.0 1.3 dynamic-slice
  50.9 0.1 copy.19
  51.0 4.6 eq.31.clone
  55.6 3.7 eq.32
  59.3 0.4 fusion.32
  59.8 0.9 fusion.45
  60.7 836.5 %all-reduce.7.cloned.1.call-done = f32[896,768]{0,1:T(8,128)} async-done(((f32[896,768]{0,1:T(8,128)}), f32[896,768]{0,1:T(8,128)}) %all-reduce.7.cloned.1.call-update) | async-done | bytes 2752528
  897.2 2.0 constant_dynamic-slice_fusion
  899.2 0.0 reduce-scatter.3.cloned.1.call-update
  899.2 0.0 all-reduce.5.cloned.1.call-start
  899.3 0.5 all-reduce.5.cloned.1.call-update
  899.8 0.2 fusion.20
  900.1 105.8 %all-reduce.1 = (f32[768]{0:T(1024)}, f32[768]{0:T(1024)}, f32[3,768]{1,0:T(4,128)}) all-reduce(f32[768]{0:T(1024)S(1)} %broadcast_multiply_fusion, f32[768]{0:T(1024)S(1)} %get-tuple-element.20, f32[3,768]{1,0:T(4,128)S(1)} %pad_maximum_fusion.6), channel_id=1, replica_groups=mesh['seq'=64,'dp'=8] {'seq','dp'}, use_global_device_ids=true, to_apply=%region_6.0 | all-reduce | flops 3840 | bytes 30720 | tf_op jit(solution)/shard_map/psum | solution.py:109
  1005.9 7.3 reduce-scatter.3.cloned.1.call-done
  1013.2 1.5 copy.16
  1014.7 349.0 %all-reduce.5.cloned.1.call-done = f32[60,768]{1,0:T(8,128)} async-done(((f32[60,768]{1,0:T(8,128)}), f32[60,768]{1,0:T(8,128)}) %all-reduce.5.cloned.1.call-update) | async-done | bytes 184336 | tf_op jit(solution)/shard_map/psum | solution.py:109
  1363.6 1.6 copy.22
  (25 shorter events, 0.2 us)
Async XLA Ops:
  8.0 11.2 copy-start
  8.0 18.5 %copy-start.4 = (f32[3,768]{1,0:T(4,128)S(1)}, f32[3,768]{1,0:T(4,128)}, u32[]{:S(2)}) copy-start(f32[3,768]{1,0:T(4,128)} %param.11) | copy-start | bytes 27652
  8.0 889.1 %all-reduce.7.cloned.1.call-start = ((), (), s32[]{:S(2)}) async-start(), calls=%async_computation.3 | async-start | bytes 5505024
  8.9 17.6 %collective-permute-start = (s32[1,7]{1,0:T(1,128)S(1)}, s32[1,7]{1,0:T(1,128)S(1)}, u32[]{:S(2)}, u32[]{:S(2)}) collective-permute-start(s32[1,7]{1,0:T(1,128)S(1)} %get-tuple-element.56), channel_id=1, source_target_pairs={{0,8},{8,16},{16,24},{24,32},{32,40},{40,48},{48,56},{56,64},{64,7... | collective-permute-start | bytes 92 | tf_op jit(solution)/shard_map/ppermute | solution.py:15
  13.9 13.1 copy-start.2
  13.9 13.1 copy-start.5
  13.9 12.8 collective-permute-start.1
  21.5 13.7 collective-permute-start.3
  23.4 11.8 collective-permute-start.2
  30.9 4.3 copy-start.3
  37.2 9.4 copy-start.1
  38.1 4.5 collective-permute-start.4
  40.7 5.9 collective-permute-start.5
  48.9 964.3 %reduce-scatter.3.cloned.1.call-start = ((), (), s32[]{:S(2)}) async-start(), calls=%async_computation.2 | async-start | bytes 442368 | tf_op jit(solution)/shard_map/reduce_scatter | solution.py:101
  899.2 464.4 %all-reduce.5.cloned.1.call-start = ((), (), s32[]{:S(2)}) async-start(), calls=%async_computation.1 | async-start | bytes 393216 | tf_op jit(solution)/shard_map/psum | solution.py:109
Sparse Core Ops, SparseCore 0:
  49.0 848.0 all-reduce.6
  901.6 111.5 reduce-scatter.2
Sparse Core Ops, SparseCore 1:
  905.7 457.8 all-reduce.4
where the time goes:
time: 1370 us
  waiting for transfers between devices  1200 us (88%)
  blocking collectives  106 us (8%)
  starting transfers between devices  19.7 us (1%)
  local copies, waits for them, and re-layouts  18.1 us (1%)
  between operations  16.5 us (1%)
    unnamed x4, waiting for transfers between devices  837 us
    psum x1, waiting for transfers between devices, local(): totals = lax.psum((g_embed, g_bias, g_gain, g_taps), ('seq', 'dp'))  349 us
    psum x1, blocking collectives, local(): totals = lax.psum((g_embed, g_bias, g_gain, g_taps), ('seq', 'dp'))  106 us
  transfers between devices with their start and end apart: 9, of which 4 were waited for; matrix products, arithmetic and copies ran while one was open for 2% of the time, Pallas kernels for 0%

commit v1 on v0

v1 whole, which is shorter than its diff:
```python
import functools

import jax
import jax.numpy as jnp
from jax import lax
from jax.experimental import pallas as pl
from jax.experimental.pallas import tpu as pltpu
from jax.sharding import PartitionSpec as P

KE = 15
DILATION_STEP = 64
C0 = 768
C1 = 896
MESH = pl.DeviceIdType.MESH
BF = jnp.bfloat16
F32 = jnp.float32
ORDER = (2, 1, 3, 0)


def device(x, y, z, core):
    return {"seq": (x * 8 + z % 8) * 2 + core, "dp": (z // 8) * 4 + y}


def reduce_kernel(
    own, oth, wid, sml,
    crecv, send1, recv1, acc1, send2, recv2, acc2,
    zsend, zrecv, ssend, srecv, fin, part,
    csem_s, csem_r, s1s, s1r, s2s, s2r, zs, zr, ss, sr, gs, gr,
):
    seq = lax.axis_index("seq")
    dp = lax.axis_index("dp")
    core = seq % 2
    x = seq // 16
    y = dp % 4
    z = (dp // 4) * 8 + (seq // 2) % 8
    zlo = z % 8
    other = 1 - core

    barrier = pltpu.get_barrier_semaphore()
    plane = [(dc, dx, dy) for dc in range(2) for dx in range(4) for dy in range(4)][1:]

    def signal(dev):
        pl.semaphore_signal(barrier, inc=1, device_id=dev, device_id_type=MESH)

    for dc, dx, dy in plane:
        signal(device((x + dx) % 4, (y + dy) % 4, z, (core + dc) % 2))
    for dz in range(1, 16):
        signal(device(x, y, (z + dz) % 16, core))
    from_y = zlo // 2

    @pl.when(from_y != y)
    def _():
        for k in range(16):
            signal(device(x, from_y, k, core))

    pl.semaphore_wait(barrier, 31 + 15 + 12)

    core_copies = []
    for o in ORDER:
        for h in range(2):
            tgt = (x + o) % 4 if h == 0 else (y + o) % 4
            c = pltpu.make_async_remote_copy(
                src_ref=oth.at[h, tgt], dst_ref=crecv.at[h, o],
                send_sem=csem_s.at[h, o], recv_sem=csem_r.at[h, o],
                device_id=device(x, y, z, other), device_id_type=MESH,
            )
            c.start()
            core_copies.append((o, h, tgt, c))

    copies1 = {}
    for o, h, tgt, c in core_copies:
        c.wait_recv()
        total = own[h, tgt] + crecv[h, o].astype(F32)
        if o == 0:
            acc1[h] = total
        else:
            send1[h, o - 1] = total.astype(BF)
            dev = device(tgt, y, z, core) if h == 0 else device(x, tgt, z, core)
            r = pltpu.make_async_remote_copy(
                src_ref=send1.at[h, o - 1], dst_ref=recv1.at[h, o - 1],
                send_sem=s1s.at[h, o - 1], recv_sem=s1r.at[h, o - 1],
                device_id=dev, device_id_type=MESH,
            )
            r.start()
            copies1[h, o] = r

    copies2 = {}
    for h in range(2):
        for o in (1, 3, 2):
            copies1[h, o].wait_recv()
        for o in ORDER:
            tgt = (y + o) % 4 if h == 0 else (x + o) % 4
            total = acc1[h, tgt]
            for k in range(3):
                total = total + recv1[h, k, tgt].astype(F32)
            if o == 0:
                acc2[h] = total
            else:
                send2[h, o - 1] = total.astype(BF)
                dev = device(x, tgt, z, core) if h == 0 else device(tgt, y, z, core)
                r = pltpu.make_async_remote_copy(
                    src_ref=send2.at[h, o - 1], dst_ref=recv2.at[h, o - 1],
                    send_sem=s2s.at[h, o - 1], recv_sem=s2r.at[h, o - 1],
                    device_id=dev, device_id_type=MESH,
                )
                r.start()
                copies2[h, o] = r

    zcopies = []
    scopies = []
    for h in range(2):
        for o in (1, 3, 2):
            copies2[h, o].wait_recv()
        total = acc2[h]
        for k in range(3):
            total = total + recv2[h, k].astype(F32)
        if h == 0:
            for i in range(6):
                part[2 * i : 2 * i + 2, :] = total[14:16, 128 * i : 128 * i + 128]
            part[12:16, :] = jnp.zeros((4, 128), F32)
            ssend[...] = part[...].astype(BF)
            for dz in range(1, 16):
                r = pltpu.make_async_remote_copy(
                    src_ref=ssend, dst_ref=srecv.at[dz - 1],
                    send_sem=ss.at[dz - 1], recv_sem=sr.at[dz - 1],
                    device_id=device(x, y, (z + dz) % 16, core), device_id_type=MESH,
                )
                r.start()
                scopies.append(r)
        for d in range(8):
            piece = total[:, 96 * d : 96 * d + 96].astype(BF)
            zsend[h, d] = jnp.concatenate([piece, jnp.zeros((16, 32), BF)], axis=1)
            to_y, to_z = d % 4, (d // 4) * 8 + 2 * y + h
            r = pltpu.make_async_remote_copy(
                src_ref=zsend.at[h, d], dst_ref=zrecv.at[z],
                send_sem=zs.at[h * 8 + d], recv_sem=zr.at[z],
                device_id=device(x, to_y, to_z, core), device_id_type=MESH,
            )
            local = pltpu.make_async_copy(zsend.at[h, d], zrecv.at[z], zr.at[z])
            mine = jnp.logical_and(to_y == y, to_z == z)
            pl.when(mine)(local.start)
            pl.when(jnp.logical_not(mine))(r.start)
            zcopies.append((mine, r))

    total = part[...]
    for k in range(15):
        scopies[k].wait_recv()
        total = total + srecv[k].astype(F32)
    fin[...] = total
    me = (core * 4 + x) * 4 + y
    sml[me] = total
    gcopies = []
    for k, (dc, dx, dy) in enumerate(plane):
        r = pltpu.make_async_remote_copy(
            src_ref=fin, dst_ref=sml.at[me],
            send_sem=gs.at[k], recv_sem=gr.at[k],
            device_id=device((x + dx) % 4, (y + dy) % 4, z, (core + dc) % 2),
            device_id_type=MESH,
        )
        r.start()
        gcopies.append(r)

    total = jnp.zeros((16, 128), F32)
    for k in range(16):
        pltpu.make_async_remote_copy(
            src_ref=zsend.at[0, 0], dst_ref=zrecv.at[k],
            send_sem=zs.at[0], recv_sem=zr.at[k],
            device_id=device(x, y, z, other), device_id_type=MESH,
        ).wait_recv()
        total = total + zrecv[k].astype(F32)
    wid[...] = total

    for k, (dc, dx, dy) in enumerate(plane):
        slot = ((core + 2 - dc) % 2 * 4 + (x + 4 - dx) % 4) * 4 + (y + 4 - dy) % 4
        pltpu.make_async_remote_copy(
            src_ref=fin, dst_ref=sml.at[slot],
            send_sem=gs.at[k], recv_sem=gr.at[k],
            device_id=device(x, y, z, other), device_id_type=MESH,
        ).wait_recv()

    for _, _, _, c in core_copies:
        c.wait_send()
    for c in list(copies1.values()) + list(copies2.values()) + scopies + gcopies:
        c.wait_send()
    for mine, r in zcopies:
        pl.when(jnp.logical_not(mine))(r.wait_send)


def reduce_all(own, oth):
    dma = pltpu.SemaphoreType.DMA
    vmem = pl.BlockSpec(memory_space=pltpu.VMEM)
    return pl.pallas_call(
        reduce_kernel,
        out_shape=(
            jax.ShapeDtypeStruct((16, 128), F32),
            jax.ShapeDtypeStruct((32, 16, 128), F32),
        ),
        in_specs=[vmem, vmem],
        out_specs=(vmem, vmem),
        scratch_shapes=[
            pltpu.VMEM((2, 4, 4, 16, C0), BF),
            pltpu.VMEM((2, 3, 4, 16, C0), BF),
            pltpu.VMEM((2, 3, 4, 16, C0), BF),
            pltpu.VMEM((2, 4, 16, C0), F32),
            pltpu.VMEM((2, 3, 16, C0), BF),
            pltpu.VMEM((2, 3, 16, C0), BF),
            pltpu.VMEM((2, 16, C0), F32),
            pltpu.VMEM((2, 8, 16, 128), BF),
            pltpu.VMEM((16, 16, 128), BF),
            pltpu.VMEM((16, 128), BF),
            pltpu.VMEM((15, 16, 128), BF),
            pltpu.VMEM((16, 128), F32),
            pltpu.VMEM((16, 128), F32),
            dma((2, 4)), dma((2, 4)),
            dma((2, 3)), dma((2, 3)),
            dma((2, 3)), dma((2, 3)),
            dma((16,)), dma((16,)),
            dma((15,)), dma((15,)),
            dma((31,)), dma((31,)),
        ],
        compiler_params=pltpu.CompilerParams(
            collective_id=0, has_side_effects=True, vmem_limit_bytes=40 * 1024 * 1024
        ),
        name="reduce_all",
    )(own, oth)


def padded(block, sides, width):
    for axis, dim in sides:
        count = lax.axis_size(axis)
        forward = [(i, i + 1) for i in range(count - 1)]
        backward = [(target, source) for source, target in forward]
        low = lax.ppermute(
            lax.slice_in_dim(block, block.shape[dim] - width, None, axis=dim), axis, forward
        )
        high = lax.ppermute(lax.slice_in_dim(block, 0, width, axis=dim), axis, backward)
        block = jnp.concatenate([low, block, high], axis=dim)
    return block


def make_patches(extended, length):
    window = jnp.stack([extended[j : j + length] for j in range(KE)], axis=1)
    table = window[:, :, None] == jnp.arange(1, 5, dtype=jnp.int32)[None, None, :]
    return table.reshape(length, KE * 4).astype(jnp.bfloat16)


def norm_gelu(value_entries, gain):
    meansq = jnp.mean(value_entries * value_entries, axis=-1, keepdims=True)
    return jax.nn.gelu(value_entries * lax.rsqrt(meansq + 1e-06) * gain)


def shifted_sum(padded_input, rows, element_count):
    step = DILATION_STEP
    total = rows[1] * padded_input[step : step + element_count].astype(F32)
    total = total + rows[0] * padded_input[0:element_count].astype(F32)
    return total + rows[2] * padded_input[2 * step : 2 * step + element_count].astype(F32)


def tap_sums(grad, padded_input, element_count):
    g = grad.astype(F32)
    step = DILATION_STEP
    return jnp.stack(
        [
            jnp.sum(g * padded_input[k * step : k * step + element_count].astype(F32), axis=0)
            for k in range(3)
        ]
    )


def with_rims(value_entries):
    return padded(value_entries, (("seq", 0),), DILATION_STEP)


def halves(g, smalls):
    g = g.reshape(4, 4, 2, 2, 14, C0)
    g = g.transpose(3, 2, 0, 1, 4, 5)
    s = smalls.reshape(2, 1, 4, 4, 2, C0)
    s = jnp.concatenate([s, jnp.zeros_like(s)], axis=1)
    g = jnp.concatenate([g, s], axis=4)
    return jnp.stack([g[:, 0], g[:, 1].transpose(0, 2, 1, 3, 4)], axis=1)


def local(bases, w_embed, b_embed, gain, taps, w_widen, cotangent):
    length = bases.shape[1]
    element_count = length // 2
    width = w_embed.shape[1]
    extended = padded(bases + 1, (("seq", 1),), KE // 2)[0]
    patches = make_patches(extended, length)
    embedded = jnp.dot(patches, w_embed, preferred_element_type=F32) + b_embed
    pooled = (jnp.sum(embedded.reshape(element_count, 2, width), axis=1) * 0.5).astype(BF)
    act_f, pull = jax.vjp(norm_gelu, pooled.astype(F32), gain)
    activation_rows = act_f.astype(BF)
    cot = cotangent[0]
    block_gradient = lax.dot_general(
        cot, w_widen, (((1,), (1,)), ((), ())), preferred_element_type=F32
    ).astype(BF)
    activation_padded = with_rims(activation_rows)
    mixed = shifted_sum(activation_padded, taps, element_count)
    padded_gradient = with_rims(block_gradient)
    g_taps = tap_sums(block_gradient, activation_padded, element_count)
    d_act = shifted_sum(padded_gradient, taps[::-1], element_count)
    block = (pooled.astype(F32) + mixed).astype(BF)
    g = lax.dot_general(cot, block, (((0,), (0,)), ((), ())), preferred_element_type=F32)
    d_norm, g_gain = pull(d_act)
    half = ((block_gradient.astype(F32) + d_norm) * 0.5).astype(BF)
    paired = jnp.sum(patches.reshape(element_count, 2, KE * 4), axis=1)
    g_embed = lax.dot_general(
        paired, half, (((0,), (0,)), ((), ())), preferred_element_type=F32
    )
    smalls = jnp.concatenate([g_embed, g_gain[None], g_taps], axis=0)
    both = halves(g, smalls)
    core = lax.axis_index("seq") % 2
    own = lax.dynamic_index_in_dim(both, core, 0, keepdims=False)
    oth = lax.dynamic_index_in_dim(both, 1 - core, 0, keepdims=False).astype(BF)
    wid, sml = reduce_all(own, oth)
    g_widen = wid[:14, :96].T
    small = sml[:, :12].reshape(32, 6, 2, 128).transpose(0, 2, 1, 3).reshape(64, C0)
    g_embed = small[:60]
    return (g_embed, jnp.sum(g_embed[28:32], axis=0), small[60], small[61:64], g_widen)


def solution(mesh):
    return jax.shard_map(
        local,
        mesh=mesh,
        in_specs=(P("dp", "seq"), P(), P(), P(), P(), P(), P("dp", "seq", None)),
        out_specs=(P(), P(), P(), P(), P("dp", "seq")),
        check_vma=False,
    )
```

time: 1370 us -> 132 us (0.10)
  waiting for transfers between devices: 1200 us -> 2.88 us
  blocking collectives: 106 us -> 0 us
  Pallas kernels: 0 us -> 66.2 us
  between operations: 16.5 us -> 1.04 us
    unnamed x4 -> x0, waiting for transfers between devices: 837 us -> none
    psum x1 -> x0, waiting for transfers between devices: 349 us -> none  [local(): totals = lax.psum((g_embed, g_bias, g_gain, g_taps), ('seq', 'dp'))]
    psum x1 -> x0, blocking collectives: 106 us -> none  [local(): totals = lax.psum((g_embed, g_bias, g_gain, g_taps), ('seq', 'dp'))]
    pallas_call x0 -> x1, Pallas kernels: none -> 66.2 us  [reduce_all(): pl.pallas_call(reduce_kernel, out_shape=(jax.ShapeDtypeStruct((16, 128),...]
  transfers between devices with their start and end apart: 9 -> 6, of which waited for: 4 -> 1; matrix products, arithmetic and copies ran while one was open for 2% -> 16% of each run, Pallas kernels for 0% -> 0%
where the time goes in v1:
time: 132 us; the launch traced here: 131 us
  Pallas kernels  66.2 us (50%)
  local copies, waits for them, and re-layouts  25.4 us (19%)
  starting transfers between devices  19.5 us (15%)
  other arithmetic  8.46 us (6%)
  matrix products  7.46 us (6%)
  waiting for transfers between devices  2.88 us (2%)
    pallas_call x1, Pallas kernels, reduce_all(): pl.pallas_call(reduce_kernel, out_shape=(jax.ShapeDtypeStruct((16, 128),...  66.2 us
    ppermute x3, starting transfers between devices, padded(): lax.ppermute(lax.slice_in_dim(block, 0, width, axis=dim), axis, backward)  10.1 us
    ppermute x3, starting transfers between devices, padded(): lax.ppermute(lax.slice_in_dim(block, block.shape[dim] - width, None, axis...  9.37 us
    eq x6, local copies, waits for them, and re-layouts, make_patches(): window[:, :, None] == jnp.arange(1, 5, dtype=jnp.int32)[None, None, :]  8.48 us
    reshape x2, local copies, waits for them, and re-layouts, halves(): g = g.reshape(4, 4, 2, 2, 14, C0)  6.1 us
    dot_general x1, local copies, waits for them, and re-layouts, local(): lax.dot_general(cot, block, (((0,), (0,)), ((), ())), preferred_element_t...  3.36 us
    dot_general x1, matrix products, local(): lax.dot_general(cot, block, (((0,), (0,)), ((), ())), preferred_element_t...  3.36 us
    reduce_sum x1, other arithmetic, local(): jnp.sum(embedded.reshape(element_count, 2, width), axis=1) * 0.5  3.31 us
  transfers between devices with their start and end apart: 6, of which 1 were waited for; matrix products, arithmetic and copies ran while one was open for 16% of the time, Pallas kernels for 0%

profile of v1, /device:TPU:1, one launch (start us, length us, event | category | flops | bytes accessed | tf_op | source)
XLA Modules:
  0.0 130.9 jit_solution(6367577945516118326)
XLA Ops:
  0.6 0.0 copy-start
  0.7 0.8 fusion.47
  1.4 0.1 fusion.51
  1.5 4.9 %collective-permute-start = (s32[1,7]{1,0:T(1,128)S(1)}, s32[1,7]{1,0:T(1,128)S(1)}, u32[]{:S(2)}, u32[]{:S(2)}) collective-permute-start(s32[1,7]{1,0:T(1,128)S(1)} %get-tuple-element.42), channel_id=1, source_target_pairs={{0,8},{8,16},{16,24},{24,32},{32,40},{40,48},{48,56},{56,64},{64,7... | collective-permute-start | bytes 92 | tf_op jit(solution)/shard_map/ppermute | solution.py:233
  6.5 0.0 copy-start.7
  6.5 5.1 %collective-permute-start.1 = (s32[1,7]{1,0:T(1,128)S(1)}, s32[1,7]{1,0:T(1,128)S(1)}, u32[]{:S(2)}, u32[]{:S(2)}) collective-permute-start(s32[1,7]{1,0:T(1,128)S(1)} %get-tuple-element.41), channel_id=1, source_target_pairs={{8,0},{16,8},{24,16},{32,24},{40,32},{48,40},{56,48},{64,56},{72,6... | collective-permute-start | bytes 92 | tf_op jit(solution)/shard_map/ppermute | solution.py:236
  11.6 1.6 %convolution_convert_fusion = bf16[256,768]{1,0:T(8,128)(2,1)S(1)} fusion(bf16[768,896]{1,0:T(8,128)(2,1)S(1)} %copy-done, bf16[1,256,896]{2,1,0:T(8,128)(2,1)} %param.13), kind=kOutput, calls=%fused_computation.24 | convolution fusion | flops 352518144 | bytes 2228224 | tf_op jit(solution)/shard_map/dot_general | solution.py:294
  13.2 0.7 fusion.50
  13.9 1.9 %collective-permute-start.4 = (bf16[64,768]{1,0:T(8,128)(2,1)}, bf16[64,768]{1,0:T(8,128)(2,1)}, u32[]{:S(2)}, u32[]{:S(2)}) collective-permute-start(bf16[64,768]{1,0:T(8,128)(2,1)} %get-tuple-element.25), channel_id=1, source_target_pairs={{0,8},{8,16},{16,24},{24,32},{32,40},{40,48},{48,56},{56,64},{64,7... | collective-permute-start | bytes 294920 | tf_op jit(solution)/shard_map/ppermute | solution.py:233
  15.9 3.0 %collective-permute-start.5 = (bf16[64,768]{1,0:T(8,128)(2,1)}, bf16[64,768]{1,0:T(8,128)(2,1)}, u32[]{:S(2)}, u32[]{:S(2)}) collective-permute-start(bf16[64,768]{1,0:T(8,128)(2,1)} %get-tuple-element.26), channel_id=1, source_target_pairs={{8,0},{16,8},{24,16},{32,24},{40,32},{48,40},{56,48},{64,56},{72,6... | collective-permute-start | bytes 294920 | tf_op jit(solution)/shard_map/ppermute | solution.py:236
  18.9 0.1 eq.36
  19.1 0.1 fusion.42
  19.2 0.1 add_bitcast_fusion
  19.3 0.1 fusion.43
  19.4 0.1 stack.78
  19.4 0.9 copy.15
  20.4 1.4 %convolution_add_fusion = f32[512,768]{1,0:T(8,128)S(1)} fusion(bf16[60,768]{1,0:T(8,128)(2,1)} %param.8, f32[768]{0:T(1024)S(1)} %copy-done.7, s32[512,60]{0,1:T(8,128)S(1)} %eq.34, s32[60]{0:T(128)S(1)} %eq.36), kind=kOutput, calls=%fused_computation.23 | convolution fusion | flops 47609856 | bytes 1791216 | tf_op jit(solution)/shard_map/dot_general | solution.py:289
  21.8 2.1 %reshape.97 = f32[256,2,768]{2,1,0:T(2,128)} reshape(f32[512,768]{1,0:T(8,128)S(1)} %convolution_add_fusion) | data formatting | bytes 3145728 | tf_op jit(solution)/shard_map/reshape | solution.py:290
  23.9 3.3 %reduce_sum.94 = f32[256,768]{1,0:T(8,128)S(1)} reduce(f32[256,2,768]{2,1,0:T(2,128)} %reshape.97, f32[]{:T(128)} %constant.21.clone.1), dimensions={1}, to_apply=%region_0.0 | reduce | flops 196608 | bytes 2359300 | tf_op jit(solution)/shard_map/reduce_sum | solution.py:290
  27.2 0.2 fusion.20
  27.4 4.6 %eq.33 = s32[512,15,4]{2,1,0:T(8,128)} broadcast(s32[512,15]{1,0:T(8,128)S(1)} %copy-done.1), dimensions={0,1} | broadcast | bytes 153600 | tf_op jit(solution)/shard_map/eq | solution.py:243
  32.0 3.7 %eq.39 = s32[256,2,60]{2,1,0:T(2,128)S(1)} reshape(s32[512,15,4]{2,1,0:T(8,128)} %eq.33) | data formatting | bytes 245760 | tf_op jit(solution)/shard_map/eq | solution.py:243
  35.7 0.4 fusion.39
  36.2 2.0 %fusion.14 = (f32[768]{0:T(1024)S(1)}, f32[256]{0:T(256)S(1)}, f32[256,768]{1,0:T(8,128)S(1)}, bf16[256,768]{1,0:T(8,128)(2,1)S(1)}) fusion(bf16[256,768]{1,0:T(8,128)(2,1)S(1)} %get-tuple-element.19, f32[256]{0:T(256)S(1)} %fusion.44, f32[768]{0:T(1024)S(1)} %copy-done.4, bf16[64,768]{1,0:T(8,128)(2,1)} %collective-permute-done.5, ...), kind=kLoop, calls=%fused_computation.41 | loop fusion | flops 8453120 | bytes 2180096 | tf_op jit(solution)/shard_map/transpose(jvp())/reduce_sum | solution.py:249
  38.3 2.5 %collective-permute-start.2 = (bf16[64,768]{1,0:T(8,128)(2,1)S(1)}, bf16[64,768]{1,0:T(8,128)(2,1)S(1)}, u32[]{:S(2)}, u32[]{:S(2)}) collective-permute-start(bf16[64,768]{1,0:T(8,128)(2,1)S(1)} %get-tuple-element.23), channel_id=1, source_target_pairs={{0,8},{8,16},{16,24},{24,32},{32,40},{40,48},{48,56},{56,64},{64,7... | collective-permute-start | bytes 294920 | tf_op jit(solution)/shard_map/ppermute | solution.py:233
  40.8 1.9 %collective-permute-start.3 = (bf16[64,768]{1,0:T(8,128)(2,1)S(1)}, bf16[64,768]{1,0:T(8,128)(2,1)S(1)}, u32[]{:S(2)}, u32[]{:S(2)}) collective-permute-start(bf16[64,768]{1,0:T(8,128)(2,1)S(1)} %get-tuple-element.24), channel_id=1, source_target_pairs={{8,0},{16,8},{24,16},{32,24},{40,32},{48,40},{56,48},{64,56},{72,6... | collective-permute-start | bytes 294920 | tf_op jit(solution)/shard_map/ppermute | solution.py:236
  42.7 1.1 fusion.37
  43.9 2.9 %collective-permute-done.3 = bf16[64,768]{1,0:T(8,128)(2,1)S(1)} collective-permute-done((bf16[64,768]{1,0:T(8,128)(2,1)S(1)}, bf16[64,768]{1,0:T(8,128)(2,1)S(1)}, u32[]{:S(2)}, u32[]{:S(2)}) %collective-permute-start.3) | collective-permute-done | bytes 98336 | tf_op jit(solution)/shard_map/ppermute | solution.py:236
  46.7 0.2 fusion.29
  47.0 0.4 copy-done.3
  47.4 0.1 reshape.100
  47.5 3.4 %convolution_bitcast_fusion = f32[896,768]{0,1:T(8,128)} fusion(bf16[1,256,896]{2,1,0:T(8,128)(2,1)} %param.13, bf16[256,768]{1,0:T(8,128)(2,1)S(1)} %get-tuple-element.22, bf16[256,768]{1,0:T(8,128)(2,1)S(1)} %get-tuple-element.19, bf16[64,768]{1,0:T(8,128)(2,1)} %copy-done.3, bf16[64,768]{1,0:T(8,128)(2,1)} %copy-done.2, f32[768]{0:T(1024)S(1)} %get-tuple-element.15, ...), kind=kOutput, calls=%fused_computation.7 | convolution fusion | flops 355663872 | bytes 4203520 | tf_op jit(solution)/shard_map/dot_general | solution.py:303
  50.9 3.4 %copy.17 = f32[896,768]{1,0:T(8,128)} copy(f32[896,768]{0,1:T(8,128)} %convolution_bitcast_fusion) | data formatting | bytes 5505024 | tf_op jit(solution)/shard_map/dot_general | solution.py:303
  54.3 4.0 %reshape.98 = f32[4,4,2,2,14,768]{5,4,3,2,1,0:T(8,128)} reshape(f32[896,768]{1,0:T(8,128)} %copy.17) | data formatting | bytes 5505024 | tf_op jit(solution)/shard_map/reshape | solution.py:275
  58.3 2.1 %copy.35 = f32[4,4,2,2,14,768]{5,4,0,1,3,2:T(8,128)S(1)} copy(f32[4,4,2,2,14,768]{5,4,3,2,1,0:T(8,128)} %reshape.98) | data formatting | bytes 5505024 | tf_op jit(solution)/shard_map/reshape | solution.py:275
  60.4 0.4 select_maximum_fusion
  60.8 0.2 slice_bitcast_fusion
  61.0 0.1 fusion.30.oth
  61.1 0.1 fusion.3.own
  61.2 66.2 %reduce_all.1 = (f32[16,128]{1,0:T(8,128)S(1)}, f32[32,16,128]{2,1,0:T(8,128)S(1)}) custom-call(f32[2,4,4,16,768]{4,3,2,1,0:T(8,128)S(1)} %fusion.3.own, bf16[2,4,4,16,768]{4,3,2,1,0:T(8,128)(2,1)S(1)} %fusion.30.oth), custom_call_target="tpu_custom_call" | custom-call | tf_op jit(solution)/shard_map/reduce_all/pallas_call | solution.py:192
  127.4 0.1 copy.21
  127.5 0.1 copy.23
  127.7 0.6 slice.223
  128.3 0.6 slice_reduce_fusion.1
  128.9 0.6 slice_reduce_fusion
  129.5 0.1 copy.22
  129.6 0.7 copy.25
  130.3 0.6 slice_bitcast_fusion.1
  (33 shorter events, 0.3 us)
Async XLA Ops:
  0.6 11.0 %copy-start = (bf16[768,896]{1,0:T(8,128)(2,1)S(1)}, bf16[768,896]{1,0:T(8,128)(2,1)}, u32[]{:S(2)}) copy-start(bf16[768,896]{1,0:T(8,128)(2,1)} %param.12) | copy-start | bytes 4128772
  0.6 18.4 %copy-start.6 = (f32[3,768]{1,0:T(4,128)S(1)}, f32[3,768]{1,0:T(4,128)}, u32[]{:S(2)}) copy-start(f32[3,768]{1,0:T(4,128)} %param.11) | copy-start | bytes 27652
  1.5 17.7 %collective-permute-start = (s32[1,7]{1,0:T(1,128)S(1)}, s32[1,7]{1,0:T(1,128)S(1)}, u32[]{:S(2)}, u32[]{:S(2)}) collective-permute-start(s32[1,7]{1,0:T(1,128)S(1)} %get-tuple-element.42), channel_id=1, source_target_pairs={{0,8},{8,16},{16,24},{24,32},{32,40},{40,48},{48,56},{56,64},{64,7... | collective-permute-start | bytes 92 | tf_op jit(solution)/shard_map/ppermute | solution.py:233
  6.5 13.9 %copy-start.7 = (f32[768]{0:T(1024)S(1)}, f32[768]{0:T(1024)}, u32[]{:S(2)}) copy-start(f32[768]{0:T(1024)} %param.9) | copy-start | bytes 9220
  6.5 12.6 %collective-permute-start.1 = (s32[1,7]{1,0:T(1,128)S(1)}, s32[1,7]{1,0:T(1,128)S(1)}, u32[]{:S(2)}, u32[]{:S(2)}) collective-permute-start(s32[1,7]{1,0:T(1,128)S(1)} %get-tuple-element.41), channel_id=1, source_target_pairs={{8,0},{16,8},{24,16},{32,24},{40,32},{48,40},{56,48},{64,56},{72,6... | collective-permute-start | bytes 92 | tf_op jit(solution)/shard_map/ppermute | solution.py:236
  13.9 22.2 %collective-permute-start.4 = (bf16[64,768]{1,0:T(8,128)(2,1)}, bf16[64,768]{1,0:T(8,128)(2,1)}, u32[]{:S(2)}, u32[]{:S(2)}) collective-permute-start(bf16[64,768]{1,0:T(8,128)(2,1)} %get-tuple-element.25), channel_id=1, source_target_pairs={{0,8},{8,16},{16,24},{24,32},{32,40},{40,48},{48,56},{56,64},{64,7... | collective-permute-start | bytes 294920 | tf_op jit(solution)/shard_map/ppermute | solution.py:233
  15.9 20.3 %collective-permute-start.5 = (bf16[64,768]{1,0:T(8,128)(2,1)}, bf16[64,768]{1,0:T(8,128)(2,1)}, u32[]{:S(2)}, u32[]{:S(2)}) collective-permute-start(bf16[64,768]{1,0:T(8,128)(2,1)} %get-tuple-element.26), channel_id=1, source_target_pairs={{8,0},{16,8},{24,16},{32,24},{40,32},{48,40},{56,48},{64,56},{72,6... | collective-permute-start | bytes 294920 | tf_op jit(solution)/shard_map/ppermute | solution.py:236
  23.9 3.5 %copy-start.1 = (s32[512,15]{1,0:T(8,128)S(1)}, s32[512,15]{1,0:T(8,128)}, u32[]{:S(2)}) copy-start(s32[512,15]{1,0:T(8,128)} %copy.15) | copy-start | bytes 92164
  27.4 8.8 %copy-start.5 = (f32[256]{0:T(256)}, f32[256]{0:T(256)S(1)}, u32[]{:S(2)}) copy-start(f32[256]{0:T(256)S(1)} %fusion.44) | copy-start | bytes 3076
  32.0 4.2 %copy-start.4 = (f32[768]{0:T(1024)S(1)}, f32[768]{0:T(1024)}, u32[]{:S(2)}) copy-start(f32[768]{0:T(1024)} %param.10) | copy-start | bytes 9220
  38.3 5.6 %collective-permute-start.2 = (bf16[64,768]{1,0:T(8,128)(2,1)S(1)}, bf16[64,768]{1,0:T(8,128)(2,1)S(1)}, u32[]{:S(2)}, u32[]{:S(2)}) collective-permute-start(bf16[64,768]{1,0:T(8,128)(2,1)S(1)} %get-tuple-element.23), channel_id=1, source_target_pairs={{0,8},{8,16},{16,24},{24,32},{32,40},{40,48},{48,56},{56,64},{64,7... | collective-permute-start | bytes 294920 | tf_op jit(solution)/shard_map/ppermute | solution.py:233
  40.8 5.9 %collective-permute-start.3 = (bf16[64,768]{1,0:T(8,128)(2,1)S(1)}, bf16[64,768]{1,0:T(8,128)(2,1)S(1)}, u32[]{:S(2)}, u32[]{:S(2)}) collective-permute-start(bf16[64,768]{1,0:T(8,128)(2,1)S(1)} %get-tuple-element.24), channel_id=1, source_target_pairs={{8,0},{16,8},{24,16},{32,24},{40,32},{48,40},{56,48},{64,56},{72,6... | collective-permute-start | bytes 294920 | tf_op jit(solution)/shard_map/ppermute | solution.py:236
  43.9 3.1 %copy-start.2 = (bf16[64,768]{1,0:T(8,128)(2,1)}, bf16[64,768]{1,0:T(8,128)(2,1)S(1)}, u32[]{:S(2)}) copy-start(bf16[64,768]{1,0:T(8,128)(2,1)S(1)} %collective-permute-done.2) | copy-start | bytes 294916
  46.7 0.6 copy-start.3

commit v2 on v1

v2 whole, which is shorter than its diff:
```python
import jax
import jax.numpy as jnp
from jax import lax
from jax.experimental import pallas as pl
from jax.experimental.pallas import tpu as pltpu
from jax.sharding import PartitionSpec as P

KE = 15
STEP = 64
C0 = 768
C1 = 896
BINS = 256
ROWS = BINS + 2 * STEP
TILES = 24
MESH = pl.DeviceIdType.MESH
BF = jnp.bfloat16
F32 = jnp.float32
ORDER = (2, 1, 3, 0)
PLANE = [(dc, dx, dy) for dc in range(2) for dx in range(4) for dy in range(4)][1:]
GELU_A = 0.7978845608028654
GELU_B = 0.044715


def device(x, y, z, core):
    return {"seq": (x * 8 + z % 8) * 2 + core, "dp": (z // 8) * 4 + y}


def dot(a, b, ca, cb):
    return lax.dot_general(a, b, (((ca,), (cb,)), ((), ())), preferred_element_type=F32)


def iota(shape, dim):
    return lax.broadcasted_iota(jnp.int32, shape, dim)


def chosen(shape, cond):
    return jnp.where(cond, jnp.ones(shape, F32), jnp.zeros(shape, F32)).astype(BF)


def column_choice(h, core):
    j = iota((256, 1), 0)
    a, b, i = j >> 6, (j >> 4) & 3, j & 15
    x, yq = (a, b) if h == 0 else (b, a)
    col = ((x * 8 + yq * 2 + h) * 2 + core) * 14 + i
    col = jnp.where(i < 14, col, -1)
    return chosen((256, C1), iota((256, C1), 1) == col)


def normed(pooled, gain):
    xf = pooled.astype(F32)
    rs = lax.rsqrt(jnp.mean(xf * xf, axis=-1, keepdims=True) + 1e-06)
    y = xf * rs
    n = y * gain
    t = jnp.tanh(GELU_A * (n + GELU_B * (n * n * n)))
    return rs, y, n, t


def fold(v):
    return v[0:8] + v[8:16]


def kernel(
    bases, w_embed, b_embed, gain, taps, w_widen, cot,
    o_embed, o_bias, o_gain, o_taps, o_widen,
    lb, rb, lcot, rcot, tt, paired, emb, pool, act, dblk, block, half, cot_t, sm, smb,
    own, oth, crecv, send1, recv1, acc1, send2, recv2, acc2, zsend, zrecv,
    rsrecv, part, ssend, srecv, fin, agb,
    hs, hr, csem_s, csem_r, s1s, s1r, s2s, s2r, zs, zr, rss, rsr, ss, sr, gs, gr,
):
    seq = lax.axis_index("seq")
    dp = lax.axis_index("dp")
    core = seq % 2
    x = seq // 16
    y = dp % 4
    z = (dp // 4) * 8 + (seq // 2) % 8
    other = 1 - core
    me = (core * 4 + x) * 4 + y
    reducer = me < TILES
    right = {"seq": (seq + 1) % 64, "dp": dp}
    left = {"seq": (seq + 63) % 64, "dp": dp}

    barrier = pltpu.get_barrier_semaphore()

    def signal(dev):
        pl.semaphore_signal(barrier, inc=1, device_id=dev, device_id_type=MESH)

    signal(right)
    signal(left)
    for dz in range(1, 16):
        signal(device(x, y, (z + dz) % 16, core))
    from_y = (z % 8) // 2

    @pl.when(from_y != y)
    def _():
        for k in range(16):
            signal(device(x, from_y, k, core))

    for dc, dx, dy in PLANE:
        signal(device((x + dx) % 4, (y + dy) % 4, z, (core + dc) % 2))

    def remote(src, dst, send, recv, dev):
        return pltpu.make_async_remote_copy(
            src_ref=src, dst_ref=dst, send_sem=send, recv_sem=recv,
            device_id=dev, device_id_type=MESH,
        )

    dblk[STEP : STEP + BINS] = dot(cot[0], w_widen[...], 1, 1).astype(BF)
    for w in range(2):
        for h in range(2):
            pick = column_choice(h, core if w == 0 else other)
            cot_t[w, h] = dot(pick, cot[0], 1, 1).astype(BF)

    pl.semaphore_wait(barrier, 2 + 31 + 15 + 12)

    halo = [
        remote(bases, lb, hs.at[0], hr.at[0], right),
        remote(bases, rb, hs.at[1], hr.at[1], left),
        remote(cot.at[0, pl.ds(BINS - STEP, STEP)], lcot, hs.at[2], hr.at[2], right),
        remote(cot.at[0, pl.ds(0, STEP)], rcot, hs.at[3], hr.at[3], left),
    ]
    for c in halo:
        c.start()
    halo[0].wait_recv()
    halo[1].wait_recv()

    ext = jnp.concatenate([lb[:, 256:512], bases[...], rb[:, 0:256]], axis=1)
    pos = iota((1, 1024), 1) + seq * 512 - 256
    ext = jnp.where(jnp.logical_and(pos >= 0, pos < 32768), ext, -1).astype(F32)
    for m in range(16):
        tt[m : m + 1, :] = pltpu.roll(ext, 1024 - 121 - m, 1)
    p, col = iota((C0, ROWS), 0), iota((C0, ROWS), 1)
    spot = jnp.where(col < 256, col + 64, jnp.where(col < 320, col - 256, col))
    even = chosen((C0, ROWS), p == 2 * spot)
    win = dot(tt[:, 0:C0].astype(BF), even, 1, 0).astype(BF)
    tap_of, base_of = iota((KE * 4, 16), 0) >> 2, (iota((KE * 4, ROWS), 0) & 3).astype(F32)
    at = iota((KE * 4, 16), 1)
    first = dot(chosen((KE * 4, 16), at == tap_of), win, 1, 0)
    second = dot(chosen((KE * 4, 16), at == tap_of + 1), win, 1, 0)
    one, zero = jnp.ones((KE * 4, ROWS), F32), jnp.zeros((KE * 4, ROWS), F32)
    paired[...] = (
        jnp.where(first == base_of, one, zero) + jnp.where(second == base_of, one, zero)
    ).astype(BF)
    emb[...] = dot(paired[...], w_embed[...], 0, 0)

    def forward(i, _):
        rows = pl.ds(pl.multiple_of(i * 16, 16), 16)
        v = (emb[rows] * 0.5 + b_embed[...]).astype(BF)
        pool[rows] = v
        _, _, n, t = normed(v, gain[...])
        to = pl.ds(pl.multiple_of(i * 16 + STEP, 16), 16)
        act[to] = (0.5 * n * (1.0 + t)).astype(BF)
        return 0

    lax.fori_loop(0, BINS // 16, forward, 0)
    has_left = jnp.where(seq > 0, 1.0, 0.0)
    has_right = jnp.where(seq < 63, 1.0, 0.0)

    def forward_rim(i, _):
        rows = pl.ds(pl.multiple_of(i * 16 + BINS, 16), 16)
        v = (emb[rows] * 0.5 + b_embed[...]).astype(BF)
        _, _, n, t = normed(v, gain[...])
        keep = jnp.where(i < 4, has_left, has_right)
        to = pl.ds(pl.multiple_of(jnp.where(i < 4, i * 16, i * 16 + BINS), 16), 16)
        act[to] = (0.5 * n * (1.0 + t) * keep).astype(BF)
        return 0

    lax.fori_loop(0, 8, forward_rim, 0)

    def mix(i, _):
        rows = pl.ds(pl.multiple_of(i * 16, 16), 16)
        total = pool[rows].astype(F32)
        for k in (1, 0, 2):
            from_ = pl.ds(pl.multiple_of(i * 16 + k * STEP, 16), 16)
            total = total + taps[k : k + 1] * act[from_].astype(F32)
        block[rows] = total.astype(BF)
        return 0

    lax.fori_loop(0, BINS // 16, mix, 0)

    core_copies = []
    for h in range(2):
        oth[h] = dot(cot_t[1, h], block[...], 1, 0).astype(BF).reshape(4, 4, 16, C0)
        for o in ORDER:
            tgt = (x + o) % 4 if h == 0 else (y + o) % 4
            c = remote(
                oth.at[h, tgt], crecv.at[h, o], csem_s.at[h, o], csem_r.at[h, o],
                device(x, y, z, other),
            )
            c.start()
            core_copies.append((o, h, tgt, c))
    for h in range(2):
        own[h] = dot(cot_t[0, h], block[...], 1, 0).reshape(4, 4, 16, C0)

    halo[2].wait_recv()
    halo[3].wait_recv()
    dblk[0:STEP] = (dot(lcot[...], w_widen[...], 1, 1) * has_left).astype(BF)
    dblk[STEP + BINS : ROWS] = (dot(rcot[...], w_widen[...], 1, 1) * has_right).astype(BF)

    def backward(i, sums):
        rows = pl.ds(pl.multiple_of(i * 16, 16), 16)
        at = [pl.ds(pl.multiple_of(i * 16 + k * STEP, 16), 16) for k in range(3)]
        d = dblk[at[1]].astype(F32)
        d_act = taps[1:2] * d
        d_act = d_act + taps[0:1] * dblk[at[2]].astype(F32)
        d_act = d_act + taps[2:3] * dblk[at[0]].astype(F32)
        rs, yv, n, t = normed(pool[rows], gain[...])
        slope = 0.5 * (1.0 + t) + 0.5 * n * (1.0 - t * t) * (
            GELU_A * (1.0 + 3.0 * GELU_B * (n * n))
        )
        dn = d_act * slope
        dy = dn * gain[...]
        d_norm = rs * (dy - yv * jnp.mean(dy * yv, axis=-1, keepdims=True))
        half[rows] = ((d + d_norm) * 0.5).astype(BF)
        new = [fold(dn * yv)] + [fold(d * act[at[k]].astype(F32)) for k in range(3)]
        return tuple(a + b for a, b in zip(sums, new))

    start = tuple(jnp.zeros((8, C0), F32) for _ in range(4))
    sums = lax.fori_loop(0, BINS // 16, backward, start)
    sm[0 : KE * 4] = dot(paired[:, 0:BINS], half[...], 1, 0)
    for k in range(4):
        sm[KE * 4 + k : KE * 4 + k + 1] = jnp.sum(sums[k], axis=0, keepdims=True)
    for c in range(TILES):
        i, j = c // 6, c % 6
        smb[c] = sm[16 * i : 16 * i + 16, 128 * j : 128 * j + 128].astype(BF)

    rs_copies = []
    for k in range(TILES):
        c = (me + k) % TILES
        r = remote(
            smb.at[c], rsrecv.at[me], rss.at[k], rsr.at[me],
            device((c // 4) % 4, c % 4, z, c // 16),
        )
        if k == 0:
            stay = pltpu.make_async_copy(smb.at[c], rsrecv.at[me], rsr.at[me])
            pl.when(reducer)(stay.start)
            pl.when(jnp.logical_not(reducer))(r.start)
        else:
            r.start()
        rs_copies.append(r)

    copies1 = {}
    for o, h, tgt, c in core_copies:
        c.wait_recv()
        total = own[h, tgt] + crecv[h, o].astype(F32)
        if o == 0:
            acc1[h] = total
        else:
            send1[h, o - 1] = total.astype(BF)
            dev = device(tgt, y, z, core) if h == 0 else device(x, tgt, z, core)
            r = remote(
                send1.at[h, o - 1], recv1.at[h, o - 1], s1s.at[h, o - 1], s1r.at[h, o - 1], dev
            )
            r.start()
            copies1[h, o] = r

    copies2 = {}
    for h in range(2):
        for o in (1, 3, 2):
            copies1[h, o].wait_recv()
        for o in ORDER:
            tgt = (y + o) % 4 if h == 0 else (x + o) % 4
            total = acc1[h, tgt]
            for k in range(3):
                total = total + recv1[h, k, tgt].astype(F32)
            if o == 0:
                acc2[h] = total
            else:
                send2[h, o - 1] = total.astype(BF)
                dev = device(x, tgt, z, core) if h == 0 else device(tgt, y, z, core)
                r = remote(
                    send2.at[h, o - 1], recv2.at[h, o - 1],
                    s2s.at[h, o - 1], s2r.at[h, o - 1], dev,
                )
                r.start()
                copies2[h, o] = r

    z_small = [
        remote(
            ssend, srecv.at[dz - 1], ss.at[dz - 1], sr.at[dz - 1],
            device(x, y, (z + dz) % 16, core),
        )
        for dz in range(1, 16)
    ]

    @pl.when(reducer)
    def _():
        total = jnp.zeros((16, 128), F32)
        for k in range(32):
            remote(
                smb.at[0], rsrecv.at[k], rss.at[0], rsr.at[k], device(x, y, z, other)
            ).wait_recv()
            total = total + rsrecv[k].astype(F32)
        part[...] = total
        ssend[...] = total.astype(BF)
        for r in z_small:
            r.start()

    zcopies = []
    for h in range(2):
        for o in (1, 3, 2):
            copies2[h, o].wait_recv()
        total = acc2[h]
        for k in range(3):
            total = total + recv2[h, k].astype(F32)
        for d in range(8):
            piece = total[:, 96 * d : 96 * d + 96].astype(BF)
            zsend[h, d] = jnp.concatenate([piece, jnp.zeros((16, 32), BF)], axis=1)
            to_y, to_z = d % 4, (d // 4) * 8 + 2 * y + h
            r = remote(
                zsend.at[h, d], zrecv.at[z], zs.at[h * 8 + d], zr.at[z],
                device(x, to_y, to_z, core),
            )
            stay = pltpu.make_async_copy(zsend.at[h, d], zrecv.at[z], zr.at[z])
            mine = jnp.logical_and(to_y == y, to_z == z)
            pl.when(mine)(stay.start)
            pl.when(jnp.logical_not(mine))(r.start)
            zcopies.append((mine, r))

    gcopies = [
        remote(
            fin, agb.at[me], gs.at[k], gr.at[me],
            device((x + dx) % 4, (y + dy) % 4, z, (core + dc) % 2),
        )
        for k, (dc, dx, dy) in enumerate(PLANE)
    ]

    @pl.when(reducer)
    def _():
        total = part[...]
        for k in range(15):
            z_small[k].wait_recv()
            total = total + srecv[k].astype(F32)
        fin[...] = total.astype(BF)
        agb[me] = total.astype(BF)
        for r in gcopies:
            r.start()

    total = jnp.zeros((16, 128), F32)
    for k in range(16):
        remote(
            zsend.at[0, 0], zrecv.at[k], zs.at[0], zr.at[k], device(x, y, z, other)
        ).wait_recv()
        total = total + zrecv[k].astype(F32)
    o_widen[...] = total.T[0:96, 0:14]

    for c in range(TILES):
        r = remote(fin, agb.at[c], gs.at[0], gr.at[c], device(x, y, z, other))
        pl.when(me != c)(r.wait_recv)
    for c in range(TILES):
        i, j = c // 6, c % 6
        sm[16 * i : 16 * i + 16, 128 * j : 128 * j + 128] = agb[c].astype(F32)
    o_embed[...] = sm[0 : KE * 4]
    o_bias[...] = jnp.sum(sm[28:32], axis=0, keepdims=True)
    o_gain[...] = sm[60:61]
    o_taps[...] = sm[61:64]

    for c in halo:
        c.wait_send()
    for _, _, _, c in core_copies:
        c.wait_send()
    for c in list(copies1.values()) + list(copies2.values()) + rs_copies[1:]:
        c.wait_send()
    pl.when(jnp.logical_not(reducer))(rs_copies[0].wait_send)

    @pl.when(reducer)
    def _():
        for r in z_small + gcopies:
            r.wait_send()

    for mine, r in zcopies:
        pl.when(jnp.logical_not(mine))(r.wait_send)


def local(bases, w_embed, b_embed, gain, taps, w_widen, cotangent):
    dma = pltpu.SemaphoreType.DMA
    vmem = pl.BlockSpec(memory_space=pltpu.VMEM)
    out = pl.pallas_call(
        kernel,
        out_shape=(
            jax.ShapeDtypeStruct((KE * 4, C0), F32),
            jax.ShapeDtypeStruct((1, C0), F32),
            jax.ShapeDtypeStruct((1, C0), F32),
            jax.ShapeDtypeStruct((3, C0), F32),
            jax.ShapeDtypeStruct((96, 14), F32),
        ),
        in_specs=[vmem] * 7,
        out_specs=(vmem,) * 5,
        scratch_shapes=[
            pltpu.VMEM((1, 512), jnp.int32),
            pltpu.VMEM((1, 512), jnp.int32),
            pltpu.VMEM((STEP, C1), BF),
            pltpu.VMEM((STEP, C1), BF),
            pltpu.VMEM((16, 1024), F32),
            pltpu.VMEM((KE * 4, ROWS), BF),
            pltpu.VMEM((ROWS, C0), F32),
            pltpu.VMEM((BINS, C0), BF),
            pltpu.VMEM((ROWS, C0), BF),
            pltpu.VMEM((ROWS, C0), BF),
            pltpu.VMEM((BINS, C0), BF),
            pltpu.VMEM((BINS, C0), BF),
            pltpu.VMEM((2, 2, 256, BINS), BF),
            pltpu.VMEM((64, C0), F32),
            pltpu.VMEM((TILES, 16, 128), BF),
            pltpu.VMEM((2, 4, 4, 16, C0), F32),
            pltpu.VMEM((2, 4, 4, 16, C0), BF),
            pltpu.VMEM((2, 4, 4, 16, C0), BF),
            pltpu.VMEM((2, 3, 4, 16, C0), BF),
            pltpu.VMEM((2, 3, 4, 16, C0), BF),
            pltpu.VMEM((2, 4, 16, C0), F32),
            pltpu.VMEM((2, 3, 16, C0), BF),
            pltpu.VMEM((2, 3, 16, C0), BF),
            pltpu.VMEM((2, 16, C0), F32),
            pltpu.VMEM((2, 8, 16, 128), BF),
            pltpu.VMEM((16, 16, 128), BF),
            pltpu.VMEM((32, 16, 128), BF),
            pltpu.VMEM((16, 128), F32),
            pltpu.VMEM((16, 128), BF),
            pltpu.VMEM((15, 16, 128), BF),
            pltpu.VMEM((16, 128), BF),
            pltpu.VMEM((TILES, 16, 128), BF),
            dma((4,)), dma((4,)),
            dma((2, 4)), dma((2, 4)),
            dma((2, 3)), dma((2, 3)),
            dma((2, 3)), dma((2, 3)),
            dma((16,)), dma((16,)),
            dma((TILES,)), dma((32,)),
            dma((15,)), dma((15,)),
            dma((31,)), dma((TILES,)),
        ],
        compiler_params=pltpu.CompilerParams(
            collective_id=0, has_side_effects=True, vmem_limit_bytes=48 * 1024 * 1024
        ),
        name="encoder_backward",
    )(
        bases, w_embed, b_embed.reshape(1, C0), gain.reshape(1, C0), taps, w_widen, cotangent
    )
    return (out[0], out[1].reshape(C0), out[2].reshape(C0), out[3], out[4])


def solution(mesh):
    return jax.shard_map(
        local,
        mesh=mesh,
        in_specs=(P("dp", "seq"), P(), P(), P(), P(), P(), P("dp", "seq", None)),
        out_specs=(P(), P(), P(), P(), P("dp", "seq")),
        check_vma=False,
    )
```

time: 132 us -> 65.5 us (0.50)
  starting transfers between devices: 19.5 us -> 0 us
  local copies, waits for them, and re-layouts: 25.4 us -> 7.96 us
  Pallas kernels: 66.2 us -> 55.3 us
  matrix products: 7.46 us -> 0 us
  other arithmetic: 8.46 us -> 1.21 us
  waiting for transfers between devices: 2.88 us -> 0 us
    ppermute x6 -> x0, starting transfers between devices: 19.5 us -> none  [the longest x3 10.1 us: padded(): lax.ppermute(lax.slice_in_dim(block, 0, width, axis=dim), axis, backward)]
    pallas_call x1, Pallas kernels: 66.2 us -> 55.3 us  [local(): pl.pallas_call(kernel, out_shape=(jax.ShapeDtypeStruct((KE * 4, C0), F32)...]
    eq x6 -> x0, local copies, waits for them, and re-layouts: 8.48 us -> none  [make_patches(): window[:, :, None] == jnp.arange(1, 5, dtype=jnp.int32)[None, None, :]]
    dot_general x4 -> x0, matrix products: 7.46 us -> none  [the longest x1 3.36 us: local(): lax.dot_general(cot, block, (((0,), (0,)), ((), ())), preferred_element_t...]
    reshape x5 -> x2, local copies, waits for them, and re-layouts: 8.3 us -> 1.38 us  [the longest x1 0.69 us: local(): b_embed.reshape(1, C0)]
    reduce_sum x6 -> x0, other arithmetic: 6.77 us -> none  [the longest x1 3.31 us: local(): jnp.sum(embedded.reshape(element_count, 2, width), axis=1) * 0.5]
    unnamed x19 -> x13, local copies, waits for them, and re-layouts: 1.18 us -> 6.58 us
    dot_general x1 -> x0, local copies, waits for them, and re-layouts: 3.36 us -> none  [local(): lax.dot_general(cot, block, (((0,), (0,)), ((), ())), preferred_element_t...]
  transfers between devices with their start and end apart: 6 -> 0, of which waited for: 1 -> 0; matrix products, arithmetic and copies ran while one was open for 16% -> 0% of each run, Pallas kernels for 0% -> 0%
where the time goes in v2:
time: 65.5 us; the launch traced here: 65.1 us
  Pallas kernels  55.3 us (84%)
  local copies, waits for them, and re-layouts  7.96 us (12%)
  other arithmetic  1.21 us (2%)
    pallas_call x1, Pallas kernels, local(): pl.pallas_call(kernel, out_shape=(jax.ShapeDtypeStruct((KE * 4, C0), F32)...  55.3 us
    unnamed x13, local copies, waits for them, and re-layouts  6.58 us

profile of v2, /device:TPU:1, one launch (start us, length us, event | category | flops | bytes accessed | tf_op | source)
XLA Modules:
  0.0 65.1 jit_solution(10355299803032214897)
XLA Ops:
  0.6 0.7 %reshape.22.b_embed = f32[1,768]{1,0:T(1,128)S(1)} reshape(f32[768]{0:T(1024)} %param.9) | data formatting | bytes 6144 | tf_op jit(solution)/shard_map/reshape | solution.py:435
  1.3 0.7 %reshape.23.gain = f32[1,768]{1,0:T(1,128)S(1)} reshape(f32[768]{0:T(1024)} %param.10) | data formatting | bytes 6144 | tf_op jit(solution)/shard_map/reshape | solution.py:435
  2.0 0.0 copy-start
  2.0 1.3 %copy-done = bf16[768,896]{1,0:T(8,128)(2,1)S(1)} copy-done((bf16[768,896]{1,0:T(8,128)(2,1)S(1)}, bf16[768,896]{1,0:T(8,128)(2,1)}, u32[]{:S(2)}) %copy-start) | copy-done | bytes 1376280
  3.4 0.0 copy-start.1
  3.4 1.0 %copy-done.1 = bf16[1,256,896]{2,1,0:T(8,128)(2,1)S(1)} copy-done((bf16[1,256,896]{2,1,0:T(8,128)(2,1)S(1)}, bf16[1,256,896]{2,1,0:T(8,128)(2,1)}, u32[]{:S(2)}) %copy-start.1) | copy-done | bytes 458776
  4.4 0.0 copy-start.2
  4.4 0.9 %copy-done.2 = bf16[60,768]{1,0:T(8,128)(2,1)S(1)} copy-done((bf16[60,768]{1,0:T(8,128)(2,1)S(1)}, bf16[60,768]{1,0:T(8,128)(2,1)}, u32[]{:S(2)}) %copy-start.2) | copy-done | bytes 92184
  5.3 0.0 copy-start.3
  5.3 0.7 %copy-done.3 = f32[3,768]{1,0:T(4,128)S(1)} copy-done((f32[3,768]{1,0:T(4,128)S(1)}, f32[3,768]{1,0:T(4,128)}, u32[]{:S(2)}) %copy-start.3) | copy-done | bytes 9240
  6.0 0.0 copy-start.4
  6.0 0.7 %copy-done.4 = s32[1,512]{1,0:T(1,128)S(1)} copy-done((s32[1,512]{1,0:T(1,128)S(1)}, s32[1,512]{1,0:T(1,128)}, u32[]{:S(2)}) %copy-start.4) | copy-done | bytes 2072
  6.7 55.3 %encoder_backward.1 = (f32[60,768]{1,0:T(8,128)S(1)}, f32[1,768]{1,0:T(1,128)S(1)}, f32[1,768]{1,0:T(1,128)S(1)}, f32[3,768]{1,0:T(4,128)S(1)}, f32[96,14]{1,0:T(8,128)S(1)}) custom-call(s32[1,512]{1,0:T(1,128)S(1)} %copy-done.4, bf16[60,768]{1,0:T(8,128)(2,1)S(1)} %copy-done.2, f32[1,768]{1,0:T(1,128)S(1)} %reshape.22.b_embed, f32[1,768]{1,0:T(1,128)S(1)} %reshape.23.gain, ...), custom_call_target="tpu_custom_call" | custom-call | tf_op jit(solution)/shard_map/encoder_backward/pallas_call | solution.py:377
  61.9 0.6 reduce
  62.5 0.6 reduce.1
  63.1 0.7 %copy.12 = f32[96,14]{0,1:T(8,128)} copy(f32[96,14]{1,0:T(8,128)S(1)} %get-tuple-element.19) | data formatting | bytes 10752
  63.8 0.7 %copy.15 = f32[60,768]{1,0:T(8,128)} copy(f32[60,768]{1,0:T(8,128)S(1)} %get-tuple-element.25) | data formatting | bytes 368640
  64.5 0.6 copy.16
Async XLA Ops:
  2.0 1.3 %copy-start = (bf16[768,896]{1,0:T(8,128)(2,1)S(1)}, bf16[768,896]{1,0:T(8,128)(2,1)}, u32[]{:S(2)}) copy-start(bf16[768,896]{1,0:T(8,128)(2,1)} %w_widen.1) | copy-start | bytes 4128772
  3.4 1.0 %copy-start.1 = (bf16[1,256,896]{2,1,0:T(8,128)(2,1)S(1)}, bf16[1,256,896]{2,1,0:T(8,128)(2,1)}, u32[]{:S(2)}) copy-start(bf16[1,256,896]{2,1,0:T(8,128)(2,1)} %cot.1) | copy-start | bytes 1376260
  4.4 0.9 %copy-start.2 = (bf16[60,768]{1,0:T(8,128)(2,1)S(1)}, bf16[60,768]{1,0:T(8,128)(2,1)}, u32[]{:S(2)}) copy-start(bf16[60,768]{1,0:T(8,128)(2,1)} %w_embed.1) | copy-start | bytes 276484
  5.3 0.7 %copy-start.3 = (f32[3,768]{1,0:T(4,128)S(1)}, f32[3,768]{1,0:T(4,128)}, u32[]{:S(2)}) copy-start(f32[3,768]{1,0:T(4,128)} %taps.1) | copy-start | bytes 27652
  6.0 0.7 %copy-start.4 = (s32[1,512]{1,0:T(1,128)S(1)}, s32[1,512]{1,0:T(1,128)}, u32[]{:S(2)}) copy-start(s32[1,512]{1,0:T(1,128)} %bases.1) | copy-start | bytes 6148

commit v3 on v2

--- a/solution.py
+++ b/solution.py
@@ -60,13 +60,21 @@
 
 
 def kernel(
+    h_bases, h_embed, h_bias, h_gain, h_taps, h_widen, h_cot,
+    agb, o_widen,
     bases, w_embed, b_embed, gain, taps, w_widen, cot,
-    o_embed, o_bias, o_gain, o_taps, o_widen,
     lb, rb, lcot, rcot, tt, paired, emb, pool, act, dblk, block, half, cot_t, sm, smb,
     own, oth, crecv, send1, recv1, acc1, send2, recv2, acc2, zsend, zrecv,
-    rsrecv, part, ssend, srecv, fin, agb,
-    hs, hr, csem_s, csem_r, s1s, s1r, s2s, s2r, zs, zr, rss, rsr, ss, sr, gs, gr,
+    rsrecv, part, ssend, srecv, fin, totals,
+    ins, hs, hr, csem_s, csem_r, s1s, s1r, s2s, s2r, zs, zr, rss, rsr, ss, sr, gs, gr,
 ):
+    pairs = [
+        (h_bases, bases), (h_embed, w_embed), (h_bias, b_embed), (h_gain, gain),
+        (h_taps, taps), (h_cot, cot), (h_widen, w_widen),
+    ]
+    loads = [pltpu.make_async_copy(a, b, ins.at[k]) for k, (a, b) in enumerate(pairs)]
+    for c in loads:
+        c.start()
     seq = lax.axis_index("seq")
     dp = lax.axis_index("dp")
     core = seq % 2
@@ -86,7 +94,7 @@
 
     signal(right)
     signal(left)
-    for dz in range(1, 16):
+    for dz in (8, 7, 9, 6, 10, 5, 11, 4, 12, 3, 13, 2, 14, 1, 15):
         signal(device(x, y, (z + dz) % 16, core))
     from_y = (z % 8) // 2
 
@@ -104,11 +112,69 @@
             device_id=dev, device_id_type=MESH,
         )
 
-    dblk[STEP : STEP + BINS] = dot(cot[0], w_widen[...], 1, 1).astype(BF)
-    for w in range(2):
-        for h in range(2):
-            pick = column_choice(h, core if w == 0 else other)
-            cot_t[w, h] = dot(pick, cot[0], 1, 1).astype(BF)
+    p, col = iota((C0, BINS), 0), iota((C0, BINS), 1)
+    tap_of, base_of = iota((KE * 4, 16), 0) >> 2, (iota((KE * 4, BINS), 0) & 3).astype(F32)
+    place = iota((KE * 4, 16), 1)
+    one, zero = jnp.ones((KE * 4, BINS), F32), jnp.zeros((KE * 4, BINS), F32)
+
+    def pairs_of(ext, bins):
+        for m in range(16):
+            tt[m : m + 1, :] = pltpu.roll(ext, 1024 - 121 - m, 1)
+        even = chosen((C0, BINS), p == 2 * bins + 128)
+        win = dot(tt[:, 0:C0].astype(BF), even, 1, 0).astype(BF)
+        first = dot(chosen((KE * 4, 16), place == tap_of), win, 1, 0)
+        second = dot(chosen((KE * 4, 16), place == tap_of + 1), win, 1, 0)
+        return jnp.where(first == base_of, one, zero) + jnp.where(second == base_of, one, zero)
+
+    def forward(src, dst, keep):
+        v = (emb[pl.ds(src, 16)] * 0.5 + b_row).astype(BF)
+        pool[pl.ds(dst, 16)] = v
+        _, _, n, t = normed(v, gain_row)
+        a = 0.5 * n * (1.0 + t)
+        act[pl.ds(dst, 16)] = (a if keep is None else a * keep).astype(BF)
+
+    def aligned(v):
+        return pl.multiple_of(v, 16)
+
+    def mix(i):
+        total = pool[pl.ds(aligned(i * 16 + STEP), 16)].astype(F32)
+        for k in (1, 0, 2):
+            total = total + taps[k : k + 1] * act[pl.ds(aligned(i * 16 + k * STEP), 16)].astype(F32)
+        block[pl.ds(aligned(i * 16), 16)] = total.astype(BF)
+
+    def backward(i):
+        at = [pl.ds(aligned(i * 16 + k * STEP), 16) for k in range(3)]
+        d = dblk[at[1]].astype(F32)
+        d_act = taps[1:2] * d
+        d_act = d_act + taps[0:1] * dblk[at[2]].astype(F32)
+        d_act = d_act + taps[2:3] * dblk[at[0]].astype(F32)
+        rs, yv, n, t = normed(pool[at[1]], gain_row)
+        slope = 0.5 * (1.0 + t) + 0.5 * n * (1.0 - t * t) * (
+            GELU_A * (1.0 + 3.0 * GELU_B * (n * n))
+        )
+        dn = d_act * slope
+        dy = dn * gain_row
+        d_norm = rs * (dy - yv * jnp.mean(dy * yv, axis=-1, keepdims=True))
+        half[pl.ds(aligned(i * 16), 16)] = ((d + d_norm) * 0.5).astype(BF)
+        return [fold(dn * yv)] + [fold(d * act[at[k]].astype(F32)) for k in range(3)]
+
+    for c in loads[:5]:
+        c.wait()
+    b_row = b_embed[...].reshape(1, C0)
+    gain_row = gain[...].reshape(1, C0)
+    mid = bases[...].astype(F32)
+    gap = jnp.full((1, 256), -1.0, F32)
+    paired[...] = pairs_of(jnp.concatenate([gap, mid, gap], axis=1), col)
+    emb[...] = dot(paired[...].astype(BF), w_embed[...], 0, 0)
+
+    def own_forward(i, _):
+        for k in range(2):
+            at = aligned(i * 32 + 16 * k)
+            forward(at, aligned(at + STEP), None)
+        return 0
+
+    lax.fori_loop(0, BINS // 32, own_forward, 0)
+    loads[5].wait()
 
     pl.semaphore_wait(barrier, 2 + 31 + 15 + 12)
 
@@ -120,62 +186,66 @@
     ]
     for c in halo:
         c.start()
+
+    loads[6].wait()
+    dblk[STEP : STEP + BINS] = dot(cot[0], w_widen[...], 1, 1).astype(BF)
+    for w in range(2):
+        for h in range(2):
+            pick = column_choice(h, core if w == 0 else other)
+            cot_t[w, h] = dot(pick, cot[0], 1, 1).astype(BF)
+
+    totals[...] = jnp.zeros((4, 8, C0), F32)
+
+    def add_up(news):
+        for k in range(4):
+            total = totals[k]
+            for new in news:
+                total = total + new[k]
+            totals[k] = total
+
+    def inner(i, _):
+        mix(5 + 2 * i)
+        mix(6 + 2 * i)
+        add_up([backward(5 + 2 * i), backward(6 + 2 * i)])
+        return 0
+
+    lax.fori_loop(0, 3, inner, 0)
+
     halo[0].wait_recv()
     halo[1].wait_recv()
-
+    has_left = jnp.where(seq > 0, 1.0, 0.0)
+    has_right = jnp.where(seq < 63, 1.0, 0.0)
     ext = jnp.concatenate([lb[:, 256:512], bases[...], rb[:, 0:256]], axis=1)
     pos = iota((1, 1024), 1) + seq * 512 - 256
     ext = jnp.where(jnp.logical_and(pos >= 0, pos < 32768), ext, -1).astype(F32)
-    for m in range(16):
-        tt[m : m + 1, :] = pltpu.roll(ext, 1024 - 121 - m, 1)
-    p, col = iota((C0, ROWS), 0), iota((C0, ROWS), 1)
-    spot = jnp.where(col < 256, col + 64, jnp.where(col < 320, col - 256, col))
-    even = chosen((C0, ROWS), p == 2 * spot)
-    win = dot(tt[:, 0:C0].astype(BF), even, 1, 0).astype(BF)
-    tap_of, base_of = iota((KE * 4, 16), 0) >> 2, (iota((KE * 4, ROWS), 0) & 3).astype(F32)
-    at = iota((KE * 4, 16), 1)
-    first = dot(chosen((KE * 4, 16), at == tap_of), win, 1, 0)
-    second = dot(chosen((KE * 4, 16), at == tap_of + 1), win, 1, 0)
-    one, zero = jnp.ones((KE * 4, ROWS), F32), jnp.zeros((KE * 4, ROWS), F32)
-    paired[...] = (
-        jnp.where(first == base_of, one, zero) + jnp.where(second == base_of, one, zero)
-    ).astype(BF)
-    emb[...] = dot(paired[...], w_embed[...], 0, 0)
-
-    def forward(i, _):
-        rows = pl.ds(pl.multiple_of(i * 16, 16), 16)
-        v = (emb[rows] * 0.5 + b_embed[...]).astype(BF)
-        pool[rows] = v
-        _, _, n, t = normed(v, gain[...])
-        to = pl.ds(pl.multiple_of(i * 16 + STEP, 16), 16)
-        act[to] = (0.5 * n * (1.0 + t)).astype(BF)
+    bins = jnp.where(
+        jnp.logical_or(col < 16, col >= 240), col, jnp.where(col < 128, col - 80, col + 128)
+    )
+    again = pairs_of(ext, bins)
+    lane = iota((KE * 4, BINS), 1)
+    paired[...] = jnp.where(jnp.logical_or(lane < 16, lane >= 240), again, paired[...])
+    emb[...] = dot(again.astype(BF), w_embed[...], 0, 0)
+
+    def rim_forward(i, _):
+        forward(
+            aligned(i * 16), aligned(jnp.where(i == 0, STEP, i * 16 - 16)),
+            jnp.where(i == 0, 1.0, has_left),
+        )
+        forward(
+            aligned(jnp.where(i == 4, 240, 128 + i * 16)),
+            aligned(jnp.where(i == 4, STEP + 240, STEP + BINS + i * 16)),
+            jnp.where(i == 4, 1.0, has_right),
+        )
         return 0
 
-    lax.fori_loop(0, BINS // 16, forward, 0)
-    has_left = jnp.where(seq > 0, 1.0, 0.0)
-    has_right = jnp.where(seq < 63, 1.0, 0.0)
-
-    def forward_rim(i, _):
-        rows = pl.ds(pl.multiple_of(i * 16 + BINS, 16), 16)
-        v = (emb[rows] * 0.5 + b_embed[...]).astype(BF)
-        _, _, n, t = normed(v, gain[...])
-        keep = jnp.where(i < 4, has_left, has_right)
-        to = pl.ds(pl.multiple_of(jnp.where(i < 4, i * 16, i * 16 + BINS), 16), 16)
-        act[to] = (0.5 * n * (1.0 + t) * keep).astype(BF)
+    lax.fori_loop(0, 5, rim_forward, 0)
+
+    def outer_mix(i, _):
+        mix(i)
+        mix(15 - i)
         return 0
 
-    lax.fori_loop(0, 8, forward_rim, 0)
-
-    def mix(i, _):
-        rows = pl.ds(pl.multiple_of(i * 16, 16), 16)
-        total = pool[rows].astype(F32)
-        for k in (1, 0, 2):
-            from_ = pl.ds(pl.multiple_of(i * 16 + k * STEP, 16), 16)
-            total = total + taps[k : k + 1] * act[from_].astype(F32)
-        block[rows] = total.astype(BF)
-        return 0
-
-    lax.fori_loop(0, BINS // 16, mix, 0)
+    lax.fori_loop(0, 5, outer_mix, 0)
 
     core_copies = []
     for h in range(2):
@@ -196,29 +266,14 @@
     dblk[0:STEP] = (dot(lcot[...], w_widen[...], 1, 1) * has_left).astype(BF)
     dblk[STEP + BINS : ROWS] = (dot(rcot[...], w_widen[...], 1, 1) * has_right).astype(BF)
 
-    def backward(i, sums):
-        rows = pl.ds(pl.multiple_of(i * 16, 16), 16)
-        at = [pl.ds(pl.multiple_of(i * 16 + k * STEP, 16), 16) for k in range(3)]
-        d = dblk[at[1]].astype(F32)
-        d_act = taps[1:2] * d
-        d_act = d_act + taps[0:1] * dblk[at[2]].astype(F32)
-        d_act = d_act + taps[2:3] * dblk[at[0]].astype(F32)
-        rs, yv, n, t = normed(pool[rows], gain[...])
-        slope = 0.5 * (1.0 + t) + 0.5 * n * (1.0 - t * t) * (
-            GELU_A * (1.0 + 3.0 * GELU_B * (n * n))
-        )
-        dn = d_act * slope
-        dy = dn * gain[...]
-        d_norm = rs * (dy - yv * jnp.mean(dy * yv, axis=-1, keepdims=True))
-        half[rows] = ((d + d_norm) * 0.5).astype(BF)
-        new = [fold(dn * yv)] + [fold(d * act[at[k]].astype(F32)) for k in range(3)]
-        return tuple(a + b for a, b in zip(sums, new))
-
-    start = tuple(jnp.zeros((8, C0), F32) for _ in range(4))
-    sums = lax.fori_loop(0, BINS // 16, backward, start)
-    sm[0 : KE * 4] = dot(paired[:, 0:BINS], half[...], 1, 0)
+    def outer_backward(i, _):
+        add_up([backward(i), backward(15 - i)])
+        return 0
+
+    lax.fori_loop(0, 5, outer_backward, 0)
+    sm[0 : KE * 4] = dot(paired[...].astype(BF), half[...], 1, 0)
     for k in range(4):
-        sm[KE * 4 + k : KE * 4 + k + 1] = jnp.sum(sums[k], axis=0, keepdims=True)
+        sm[KE * 4 + k : KE * 4 + k + 1] = jnp.sum(totals[k], axis=0, keepdims=True)
     for c in range(TILES):
         i, j = c // 6, c % 6
         smb[c] = sm[16 * i : 16 * i + 16, 128 * j : 128 * j + 128].astype(BF)
@@ -252,6 +307,27 @@
             )
             r.start()
             copies1[h, o] = r
+
+    z_small = [
+        remote(
+            ssend, srecv.at[dz - 1], ss.at[dz - 1], sr.at[dz - 1],
+            device(x, y, (z + dz) % 16, core),
+        )
+        for dz in range(1, 16)
+    ]
+
+    @pl.when(reducer)
+    def _():
+        total = jnp.zeros((16, 128), F32)
+        for k in range(32):
+            remote(
+                smb.at[0], rsrecv.at[k], rss.at[0], rsr.at[k], device(x, y, z, other)
+            ).wait_recv()
+            total = total + rsrecv[k].astype(F32)
+        part[...] = total
+        ssend[...] = total.astype(BF)
+        for r in z_small:
+            r.start()
 
     copies2 = {}
     for h in range(2):
@@ -274,27 +350,6 @@
                 r.start()
                 copies2[h, o] = r
 
-    z_small = [
-        remote(
-            ssend, srecv.at[dz - 1], ss.at[dz - 1], sr.at[dz - 1],
-            device(x, y, (z + dz) % 16, core),
-        )
-        for dz in range(1, 16)
-    ]
-
-    @pl.when(reducer)
-    def _():
-        total = jnp.zeros((16, 128), F32)
-        for k in range(32):
-            remote(
-                smb.at[0], rsrecv.at[k], rss.at[0], rsr.at[k], device(x, y, z, other)
-            ).wait_recv()
-            total = total + rsrecv[k].astype(F32)
-        part[...] = total
-        ssend[...] = total.astype(BF)
-        for r in z_small:
-            r.start()
-
     zcopies = []
     for h in range(2):
         for o in (1, 3, 2):
@@ -341,19 +396,11 @@
             zsend.at[0, 0], zrecv.at[k], zs.at[0], zr.at[k], device(x, y, z, other)
         ).wait_recv()
         total = total + zrecv[k].astype(F32)
-    o_widen[...] = total.T[0:96, 0:14]
+    o_widen[...] = total
 
     for c in range(TILES):
         r = remote(fin, agb.at[c], gs.at[0], gr.at[c], device(x, y, z, other))
         pl.when(me != c)(r.wait_recv)
-    for c in range(TILES):
-        i, j = c // 6, c % 6
-        sm[16 * i : 16 * i + 16, 128 * j : 128 * j + 128] = agb[c].astype(F32)
-    o_embed[...] = sm[0 : KE * 4]
-    o_bias[...] = jnp.sum(sm[28:32], axis=0, keepdims=True)
-    o_gain[...] = sm[60:61]
-    o_taps[...] = sm[61:64]
-
     for c in halo:
         c.wait_send()
     for _, _, _, c in core_copies:
@@ -371,29 +418,45 @@
         pl.when(jnp.logical_not(mine))(r.wait_send)
 
 
+def finish(agb, wid, o_embed, o_bias, o_gain, o_taps, o_widen):
+    rows = []
+    for i in range(4):
+        rows.append(jnp.concatenate([agb[6 * i + j] for j in range(6)], axis=1).astype(F32))
+    o_embed[0:48] = jnp.concatenate(rows[:3], axis=0)
+    o_embed[48:60] = rows[3][0:12]
+    o_bias[...] = jnp.sum(rows[1][12:16], axis=0, keepdims=True).reshape(C0)
+    o_gain[...] = rows[3][12:13].reshape(C0)
+    o_taps[...] = rows[3][13:16]
+    o_widen[...] = wid[...].T[0:96, 0:14]
+
+
 def local(bases, w_embed, b_embed, gain, taps, w_widen, cotangent):
     dma = pltpu.SemaphoreType.DMA
     vmem = pl.BlockSpec(memory_space=pltpu.VMEM)
-    out = pl.pallas_call(
+    agb, wid = pl.pallas_call(
         kernel,
         out_shape=(
-            jax.ShapeDtypeStruct((KE * 4, C0), F32),
-            jax.ShapeDtypeStruct((1, C0), F32),
-            jax.ShapeDtypeStruct((1, C0), F32),
-            jax.ShapeDtypeStruct((3, C0), F32),
-            jax.ShapeDtypeStruct((96, 14), F32),
+            jax.ShapeDtypeStruct((TILES, 16, 128), BF),
+            jax.ShapeDtypeStruct((16, 128), F32),
         ),
-        in_specs=[vmem] * 7,
-        out_specs=(vmem,) * 5,
+        in_specs=[pl.BlockSpec(memory_space=pltpu.HBM)] * 7,
+        out_specs=(vmem,) * 2,
         scratch_shapes=[
+            pltpu.VMEM((1, 512), jnp.int32),
+            pltpu.VMEM((KE * 4, C0), BF),
+            pltpu.VMEM((C0,), F32),
+            pltpu.VMEM((C0,), F32),
+            pltpu.VMEM((3, C0), F32),
+            pltpu.VMEM((C0, C1), BF),
+            pltpu.VMEM((1, BINS, C1), BF),
             pltpu.VMEM((1, 512), jnp.int32),
             pltpu.VMEM((1, 512), jnp.int32),
             pltpu.VMEM((STEP, C1), BF),
             pltpu.VMEM((STEP, C1), BF),
             pltpu.VMEM((16, 1024), F32),
-            pltpu.VMEM((KE * 4, ROWS), BF),
-            pltpu.VMEM((ROWS, C0), F32),
-            pltpu.VMEM((BINS, C0), BF),
+            pltpu.VMEM((KE * 4, BINS), F32),
+            pltpu.VMEM((BINS, C0), F32),
+            pltpu.VMEM((ROWS, C0), BF),
             pltpu.VMEM((ROWS, C0), BF),
             pltpu.VMEM((ROWS, C0), BF),
             pltpu.VMEM((BINS, C0), BF),
@@ -417,7 +480,8 @@
             pltpu.VMEM((16, 128), BF),
             pltpu.VMEM((15, 16, 128), BF),
             pltpu.VMEM((16, 128), BF),
-            pltpu.VMEM((TILES, 16, 128), BF),
+            pltpu.VMEM((4, 8, C0), F32),
+            dma((7,)),
             dma((4,)), dma((4,)),
             dma((2, 4)), dma((2, 4)),
             dma((2, 3)), dma((2, 3)),
@@ -431,10 +495,21 @@
             collective_id=0, has_side_effects=True, vmem_limit_bytes=48 * 1024 * 1024
         ),
         name="encoder_backward",
-    )(
-        bases, w_embed, b_embed.reshape(1, C0), gain.reshape(1, C0), taps, w_widen, cotangent
-    )
-    return (out[0], out[1].reshape(C0), out[2].reshape(C0), out[3], out[4])
+    )(bases, w_embed, b_embed, gain, taps, w_widen, cotangent)
+    out = pl.pallas_call(
+        finish,
+        out_shape=(
+            jax.ShapeDtypeStruct((KE * 4, C0), F32),
+            jax.ShapeDtypeStruct((C0,), F32),
+            jax.ShapeDtypeStruct((C0,), F32),
+            jax.ShapeDtypeStruct((3, C0), F32),
+            jax.ShapeDtypeStruct((96, 14), F32),
+        ),
+        in_specs=[vmem] * 2,
+        out_specs=(vmem,) * 5,
+        name="finish",
+    )(agb, wid)
+    return tuple(out)
 
 
 def solution(mesh):

time: 65.5 us -> 61.6 us (0.940)
  Pallas kernels: 55.3 us -> 51.8 us
  other arithmetic: 1.21 us -> 0 us
  local copies, waits for them, and re-layouts: 7.96 us -> 8.7 us
    pallas_call x1 -> x2, Pallas kernels: 55.3 us -> 51.8 us  [the longest x1 50.2 us: local(): pl.pallas_call(kernel, out_shape=(jax.ShapeDtypeStruct((TILES, 16, 128),...]
    pallas_call x0 -> x1, local copies, waits for them, and re-layouts: none -> 1.47 us  [local(): pl.pallas_call(finish, out_shape=(jax.ShapeDtypeStruct((KE * 4, C0), F32)...]
    reshape x2 -> x0, local copies, waits for them, and re-layouts: 1.38 us -> none  [the longest x1 0.69 us: local(): b_embed.reshape(1, C0)]
    pallas_call x2 -> x0, other arithmetic: 1.21 us -> none  [local(): pl.pallas_call(kernel, out_shape=(jax.ShapeDtypeStruct((KE * 4, C0), F32)...]
    unnamed x13 -> x18, local copies, waits for them, and re-layouts: 6.58 us -> 7.23 us
where the time goes in v3:
time: 61.6 us; the launch traced here: 61.1 us
  Pallas kernels  51.8 us (84%)
  local copies, waits for them, and re-layouts  8.7 us (14%)
  between operations  0.67 us (1%)
    pallas_call x1, Pallas kernels, local(): pl.pallas_call(kernel, out_shape=(jax.ShapeDtypeStruct((TILES, 16, 128),...  50.2 us
    unnamed x18, local copies, waits for them, and re-layouts  7.23 us
    pallas_call x1, Pallas kernels, local(): pl.pallas_call(finish, out_shape=(jax.ShapeDtypeStruct((KE * 4, C0), F32)...  1.6 us
    pallas_call x1, local copies, waits for them, and re-layouts, local(): pl.pallas_call(finish, out_shape=(jax.ShapeDtypeStruct((KE * 4, C0), F32)...  1.47 us

profile of v3, /device:TPU:1, one launch (start us, length us, event | category | flops | bytes accessed | tf_op | source)
XLA Modules:
  0.0 61.1 jit_solution(5364030373738731352)
XLA Ops:
  0.6 0.0 copy-start
  0.6 1.3 %copy-done = bf16[768,896]{1,0:T(8,128)(2,1)S(1)} copy-done((bf16[768,896]{1,0:T(8,128)(2,1)S(1)}, bf16[768,896]{1,0:T(8,128)(2,1)}, u32[]{:S(2)}) %copy-start) | copy-done | bytes 1376280
  2.0 0.0 copy-start.1
  2.0 1.0 %copy-done.1 = bf16[1,256,896]{2,1,0:T(8,128)(2,1)S(1)} copy-done((bf16[1,256,896]{2,1,0:T(8,128)(2,1)S(1)}, bf16[1,256,896]{2,1,0:T(8,128)(2,1)}, u32[]{:S(2)}) %copy-start.1) | copy-done | bytes 458776
  3.0 0.0 copy-start.2
  3.0 0.9 %copy-done.2 = bf16[60,768]{1,0:T(8,128)(2,1)S(1)} copy-done((bf16[60,768]{1,0:T(8,128)(2,1)S(1)}, bf16[60,768]{1,0:T(8,128)(2,1)}, u32[]{:S(2)}) %copy-start.2) | copy-done | bytes 92184
  3.9 0.0 copy-start.4
  3.9 0.7 %copy-done.4 = f32[3,768]{1,0:T(4,128)S(1)} copy-done((f32[3,768]{1,0:T(4,128)S(1)}, f32[3,768]{1,0:T(4,128)}, u32[]{:S(2)}) %copy-start.4) | copy-done | bytes 9240
  4.6 0.0 copy-start.6
  4.6 0.7 %copy-done.6 = f32[768]{0:T(1024)S(1)} copy-done((f32[768]{0:T(1024)S(1)}, f32[768]{0:T(1024)}, u32[]{:S(2)}) %copy-start.6) | copy-done | bytes 3096
  5.3 0.0 copy-start.7
  5.3 0.7 %copy-done.7 = f32[768]{0:T(1024)S(1)} copy-done((f32[768]{0:T(1024)S(1)}, f32[768]{0:T(1024)}, u32[]{:S(2)}) %copy-start.7) | copy-done | bytes 3096
  6.0 0.0 copy-start.8
  6.0 0.7 %copy-done.8 = s32[1,512]{1,0:T(1,128)S(1)} copy-done((s32[1,512]{1,0:T(1,128)S(1)}, s32[1,512]{1,0:T(1,128)}, u32[]{:S(2)}) %copy-start.8) | copy-done | bytes 2072
  6.7 50.2 %encoder_backward.1 = (bf16[24,16,128]{2,1,0:T(8,128)(2,1)S(1)}, f32[16,128]{1,0:T(8,128)S(1)}) custom-call(s32[1,512]{1,0:T(1,128)S(1)} %copy-done.8, bf16[60,768]{1,0:T(8,128)(2,1)S(1)} %copy-done.2, f32[768]{0:T(1024)S(1)} %copy-done.6, f32[768]{0:T(1024)S(1)} %copy-done.7, f32[3,768]{1,0:T(4,128)S(1)} %copy-done.4, bf16[768,896]{1,0:T(8,128)(2,1)S(1)} %copy-done, ...), custom_call_target="tpu_custom_call" | custom-call | tf_op jit(solution)/shard_map/encoder_backward/pallas_call | solution.py:436
  56.8 0.0 copy-start.3
  56.8 0.6 %copy-done.3 = bf16[24,16,128]{2,1,0:T(8,128)(2,1)} copy-done((bf16[24,16,128]{2,1,0:T(8,128)(2,1)}, bf16[24,16,128]{2,1,0:T(8,128)(2,1)S(1)}, u32[]{:S(2)}) %copy-start.3) | copy-done | bytes 98328
  57.5 0.0 copy-start.5
  57.5 0.6 copy-done.5
  58.1 1.6 %finish.1 = (f32[60,768]{1,0:T(8,128)}, f32[768]{0:T(1024)}, f32[768]{0:T(1024)}, f32[3,768]{1,0:T(4,128)}, f32[96,14]{1,0:T(8,128)}) custom-call(bf16[24,16,128]{2,1,0:T(8,128)(2,1)} %copy-done.3, f32[16,128]{1,0:T(8,128)} %copy-done.5), custom_call_target="tpu_custom_call" | custom-call | tf_op jit(solution)/shard_map/finish/pallas_call | solution.py:499
  59.7 1.5 %copy.12 = f32[96,14]{0,1:T(8,128)} copy(f32[96,14]{1,0:T(8,128)} %get-tuple-element.13) | data formatting | bytes 10752 | tf_op jit(solution)/shard_map/finish/pallas_call | solution.py:499
Async XLA Ops:
  0.6 1.3 %copy-start = (bf16[768,896]{1,0:T(8,128)(2,1)S(1)}, bf16[768,896]{1,0:T(8,128)(2,1)}, u32[]{:S(2)}) copy-start(bf16[768,896]{1,0:T(8,128)(2,1)} %h_widen.1) | copy-start | bytes 4128772
  2.0 1.0 %copy-start.1 = (bf16[1,256,896]{2,1,0:T(8,128)(2,1)S(1)}, bf16[1,256,896]{2,1,0:T(8,128)(2,1)}, u32[]{:S(2)}) copy-start(bf16[1,256,896]{2,1,0:T(8,128)(2,1)} %h_cot.1) | copy-start | bytes 1376260
  3.0 0.9 %copy-start.2 = (bf16[60,768]{1,0:T(8,128)(2,1)S(1)}, bf16[60,768]{1,0:T(8,128)(2,1)}, u32[]{:S(2)}) copy-start(bf16[60,768]{1,0:T(8,128)(2,1)} %h_embed.1) | copy-start | bytes 276484
  3.9 0.7 %copy-start.4 = (f32[3,768]{1,0:T(4,128)S(1)}, f32[3,768]{1,0:T(4,128)}, u32[]{:S(2)}) copy-start(f32[3,768]{1,0:T(4,128)} %h_taps.1) | copy-start | bytes 27652
  4.6 0.7 %copy-start.6 = (f32[768]{0:T(1024)S(1)}, f32[768]{0:T(1024)}, u32[]{:S(2)}) copy-start(f32[768]{0:T(1024)} %h_bias.1) | copy-start | bytes 9220
  5.3 0.7 %copy-start.7 = (f32[768]{0:T(1024)S(1)}, f32[768]{0:T(1024)}, u32[]{:S(2)}) copy-start(f32[768]{0:T(1024)} %h_gain.1) | copy-start | bytes 9220
  6.0 0.7 %copy-start.8 = (s32[1,512]{1,0:T(1,128)S(1)}, s32[1,512]{1,0:T(1,128)}, u32[]{:S(2)}) copy-start(s32[1,512]{1,0:T(1,128)} %h_bases.1) | copy-start | bytes 6148
  56.8 0.6 %copy-start.3 = (bf16[24,16,128]{2,1,0:T(8,128)(2,1)}, bf16[24,16,128]{2,1,0:T(8,128)(2,1)S(1)}, u32[]{:S(2)}) copy-start(bf16[24,16,128]{2,1,0:T(8,128)(2,1)S(1)} %get-tuple-element.7.agb) | copy-start | bytes 294916
  57.5 0.6 copy-start.5

commit v4 on v3

--- a/solution.py
+++ b/solution.py
@@ -427,7 +427,7 @@
     o_bias[...] = jnp.sum(rows[1][12:16], axis=0, keepdims=True).reshape(C0)
     o_gain[...] = rows[3][12:13].reshape(C0)
     o_taps[...] = rows[3][13:16]
-    o_widen[...] = wid[...].T[0:96, 0:14]
+    o_widen[...] = wid[0:14, 0:96]
 
 
 def local(bases, w_embed, b_embed, gain, taps, w_widen, cotangent):
@@ -492,7 +492,7 @@
             dma((31,)), dma((TILES,)),
         ],
         compiler_params=pltpu.CompilerParams(
-            collective_id=0, has_side_effects=True, vmem_limit_bytes=48 * 1024 * 1024
+            collective_id=0, has_side_effects=True, vmem_limit_bytes=60 * 1024 * 1024
         ),
         name="encoder_backward",
     )(bases, w_embed, b_embed, gain, taps, w_widen, cotangent)
@@ -503,13 +503,14 @@
             jax.ShapeDtypeStruct((C0,), F32),
             jax.ShapeDtypeStruct((C0,), F32),
             jax.ShapeDtypeStruct((3, C0), F32),
-            jax.ShapeDtypeStruct((96, 14), F32),
+            jax.ShapeDtypeStruct((14, 96), F32),
         ),
         in_specs=[vmem] * 2,
         out_specs=(vmem,) * 5,
+        compiler_params=pltpu.CompilerParams(vmem_limit_bytes=60 * 1024 * 1024),
         name="finish",
     )(agb, wid)
-    return tuple(out)
+    return (*out[:4], out[4].T)
 
 
 def solution(mesh):

time: 61.6 us -> 52.6 us (0.85)
  local copies, waits for them, and re-layouts: 8.7 us -> 0 us
    unnamed x18 -> x0, local copies, waits for them, and re-layouts: 7.23 us -> none
    pallas_call x1 -> x0, local copies, waits for them, and re-layouts: 1.47 us -> none  [local(): pl.pallas_call(finish, out_shape=(jax.ShapeDtypeStruct((KE * 4, C0), F32)...]
where the time goes in v4:
time: 52.6 us; the launch traced here: 52.5 us
  Pallas kernels  51.8 us (98%)
  between operations  0.64 us (1%)
    pallas_call x1, Pallas kernels, local(): pl.pallas_call(kernel, out_shape=(jax.ShapeDtypeStruct((TILES, 16, 128),...  50.2 us
    pallas_call x1, Pallas kernels, local(): pl.pallas_call(finish, out_shape=(jax.ShapeDtypeStruct((KE * 4, C0), F32)...  1.6 us

profile of v4, /device:TPU:1, one launch (start us, length us, event | category | flops | bytes accessed | tf_op | source)
XLA Modules:
  0.0 52.5 jit_solution(14839534180306391027)
XLA Ops:
  0.6 50.2 %encoder_backward.1 = (bf16[24,16,128]{2,1,0:T(8,128)(2,1)}, f32[16,128]{1,0:T(8,128)}) custom-call(s32[1,512]{1,0:T(1,128)} %h_bases.1, bf16[60,768]{1,0:T(8,128)(2,1)} %h_embed.1, f32[768]{0:T(1024)} %h_bias.1, f32[768]{0:T(1024)} %h_gain.1, f32[3,768]{1,0:T(4,128)} %h_taps.1, bf16[768,896]{1,0:T(8,128)(2,1)} %h_widen.1, bf16[1,256,896]{2,1,0:T(8,128)(2,1)} %h_cot.1), custom_call_target="tpu_custom_call" | custom-call | tf_op jit(solution)/shard_map/encoder_backward/pallas_call | solution.py:436
  50.9 1.6 %finish.1 = (f32[60,768]{1,0:T(8,128)}, f32[768]{0:T(1024)}, f32[768]{0:T(1024)}, f32[3,768]{1,0:T(4,128)}, f32[14,96]{1,0:T(8,128)}) custom-call(bf16[24,16,128]{2,1,0:T(8,128)(2,1)} %get-tuple-element.12.agb, f32[16,128]{1,0:T(8,128)} %get-tuple-element.13.wid), custom_call_target="tpu_custom_call" | custom-call | tf_op jit(solution)/shard_map/finish/pallas_call | solution.py:499

commit v5 on v4

--- a/solution.py
+++ b/solution.py
@@ -16,7 +16,8 @@
 BF = jnp.bfloat16
 F32 = jnp.float32
 ORDER = (2, 1, 3, 0)
-PLANE = [(dc, dx, dy) for dc in range(2) for dx in range(4) for dy in range(4)][1:]
+PLANE = [(dc, dx, dy) for dx in (2, 1, 3, 0) for dy in (2, 1, 3, 0) for dc in (1, 0)][:-1]
+NEAR = (4, 12, 3, 13, 2, 14, 1, 15)
 GELU_A = 0.7978845608028654
 GELU_B = 0.044715
 
@@ -63,10 +64,10 @@
     h_bases, h_embed, h_bias, h_gain, h_taps, h_widen, h_cot,
     agb, o_widen,
     bases, w_embed, b_embed, gain, taps, w_widen, cot,
-    lb, rb, lcot, rcot, tt, paired, emb, pool, act, dblk, block, half, cot_t, sm, smb,
+    lb, rb, rim, tt, paired, emb, pool, act, dblk, block, half, cot_t, sm, smb,
     own, oth, crecv, send1, recv1, acc1, send2, recv2, acc2, zsend, zrecv,
     rsrecv, part, ssend, srecv, fin, totals,
-    ins, hs, hr, csem_s, csem_r, s1s, s1r, s2s, s2r, zs, zr, rss, rsr, ss, sr, gs, gr,
+    ins, heard, hs, hr, csem_s, csem_r, s1s, s1r, s2s, s2r, zs, zr, rss, rsr, ss, sr, gs, gr,
 ):
     pairs = [
         (h_bases, bases), (h_embed, w_embed), (h_bias, b_embed), (h_gain, gain),
@@ -89,22 +90,15 @@
 
     barrier = pltpu.get_barrier_semaphore()
 
-    def signal(dev):
-        pl.semaphore_signal(barrier, inc=1, device_id=dev, device_id_type=MESH)
-
-    signal(right)
-    signal(left)
-    for dz in (8, 7, 9, 6, 10, 5, 11, 4, 12, 3, 13, 2, 14, 1, 15):
-        signal(device(x, y, (z + dz) % 16, core))
-    from_y = (z % 8) // 2
-
-    @pl.when(from_y != y)
-    def _():
-        for k in range(16):
-            signal(device(x, from_y, k, core))
-
+    def signal(sem, dev):
+        pl.semaphore_signal(sem, inc=1, device_id=dev, device_id_type=MESH)
+
+    signal(barrier, right)
+    signal(barrier, left)
+    for dz in NEAR:
+        signal(barrier, device(x, y, (z + dz) % 16, core))
     for dc, dx, dy in PLANE:
-        signal(device((x + dx) % 4, (y + dy) % 4, z, (core + dc) % 2))
+        signal(barrier, device((x + dx) % 4, (y + dy) % 4, z, (core + dc) % 2))
 
     def remote(src, dst, send, recv, dev):
         return pltpu.make_async_remote_copy(
@@ -134,7 +128,7 @@
         act[pl.ds(dst, 16)] = (a if keep is None else a * keep).astype(BF)
 
     def aligned(v):
-        return pl.multiple_of(v, 16)
+        return v if isinstance(v, int) else pl.multiple_of(v, 16)
 
     def mix(i):
         total = pool[pl.ds(aligned(i * 16 + STEP), 16)].astype(F32)
@@ -176,16 +170,18 @@
     lax.fori_loop(0, BINS // 32, own_forward, 0)
     loads[5].wait()
 
-    pl.semaphore_wait(barrier, 2 + 31 + 15 + 12)
+    pl.semaphore_wait(barrier, 2 + len(NEAR) + len(PLANE))
 
     halo = [
         remote(bases, lb, hs.at[0], hr.at[0], right),
         remote(bases, rb, hs.at[1], hr.at[1], left),
-        remote(cot.at[0, pl.ds(BINS - STEP, STEP)], lcot, hs.at[2], hr.at[2], right),
-        remote(cot.at[0, pl.ds(0, STEP)], rcot, hs.at[3], hr.at[3], left),
+        remote(cot.at[0, pl.ds(BINS - STEP, STEP)], rim.at[pl.ds(0, STEP)], hs.at[2], hr.at[2], right),
+        remote(cot.at[0, pl.ds(0, STEP)], rim.at[pl.ds(STEP, STEP)], hs.at[3], hr.at[3], left),
     ]
     for c in halo:
         c.start()
+    for dz in NEAR:
+        signal(heard.at[0], device(x, y, (z + dz) % 16, core))
 
     loads[6].wait()
     dblk[STEP : STEP + BINS] = dot(cot[0], w_widen[...], 1, 1).astype(BF)
@@ -210,6 +206,10 @@
         return 0
 
     lax.fori_loop(0, 3, inner, 0)
+
+    pl.semaphore_wait(heard.at[0], len(NEAR))
+    for dz in NEAR:
+        signal(heard.at[1], device(x, y, (z + dz) % 16, core))
 
     halo[0].wait_recv()
     halo[1].wait_recv()
@@ -226,51 +226,24 @@
     paired[...] = jnp.where(jnp.logical_or(lane < 16, lane >= 240), again, paired[...])
     emb[...] = dot(again.astype(BF), w_embed[...], 0, 0)
 
-    def rim_forward(i, _):
+    for i in range(5):
+        forward(i * 16, STEP if i == 0 else i * 16 - 16, None if i == 0 else has_left)
         forward(
-            aligned(i * 16), aligned(jnp.where(i == 0, STEP, i * 16 - 16)),
-            jnp.where(i == 0, 1.0, has_left),
+            240 if i == 4 else 128 + i * 16, STEP + 240 if i == 4 else STEP + BINS + i * 16,
+            None if i == 4 else has_right,
         )
-        forward(
-            aligned(jnp.where(i == 4, 240, 128 + i * 16)),
-            aligned(jnp.where(i == 4, STEP + 240, STEP + BINS + i * 16)),
-            jnp.where(i == 4, 1.0, has_right),
-        )
-        return 0
-
-    lax.fori_loop(0, 5, rim_forward, 0)
-
-    def outer_mix(i, _):
+
+    for i in range(5):
         mix(i)
         mix(15 - i)
-        return 0
-
-    lax.fori_loop(0, 5, outer_mix, 0)
-
-    core_copies = []
-    for h in range(2):
-        oth[h] = dot(cot_t[1, h], block[...], 1, 0).astype(BF).reshape(4, 4, 16, C0)
-        for o in ORDER:
-            tgt = (x + o) % 4 if h == 0 else (y + o) % 4
-            c = remote(
-                oth.at[h, tgt], crecv.at[h, o], csem_s.at[h, o], csem_r.at[h, o],
-                device(x, y, z, other),
-            )
-            c.start()
-            core_copies.append((o, h, tgt, c))
-    for h in range(2):
-        own[h] = dot(cot_t[0, h], block[...], 1, 0).reshape(4, 4, 16, C0)
 
     halo[2].wait_recv()
     halo[3].wait_recv()
-    dblk[0:STEP] = (dot(lcot[...], w_widen[...], 1, 1) * has_left).astype(BF)
-    dblk[STEP + BINS : ROWS] = (dot(rcot[...], w_widen[...], 1, 1) * has_right).astype(BF)
-
-    def outer_backward(i, _):
-        add_up([backward(i), backward(15 - i)])
-        return 0
-
-    lax.fori_loop(0, 5, outer_backward, 0)
+    outside = dot(rim[...], w_widen[...], 1, 1)
+    dblk[0:STEP] = (outside[0:STEP] * has_left).astype(BF)
+    dblk[STEP + BINS : ROWS] = (outside[STEP:] * has_right).astype(BF)
+
+    add_up([backward(i) for k in range(5) for i in (k, 15 - k)])
     sm[0 : KE * 4] = dot(paired[...].astype(BF), half[...], 1, 0)
     for k in range(4):
         sm[KE * 4 + k : KE * 4 + k + 1] = jnp.sum(totals[k], axis=0, keepdims=True)
@@ -293,20 +266,40 @@
             r.start()
         rs_copies.append(r)
 
+    core_copies = []
+    for h in range(2):
+        oth[h] = dot(cot_t[1, h], block[...], 1, 0).astype(BF).reshape(4, 4, 16, C0)
+    for o in ORDER:
+        for h in range(2):
+            then = (y + o) % 4 if h == 0 else (x + o) % 4
+            c = remote(
+                oth.at[h, :, then], crecv.at[h, o], csem_s.at[h, o], csem_r.at[h, o],
+                device(x, y, z, other),
+            )
+            c.start()
+            core_copies.append((o, h, then, c))
+    for h in range(2):
+        own[h] = dot(cot_t[0, h], block[...], 1, 0).reshape(4, 4, 16, C0)
+
     copies1 = {}
-    for o, h, tgt, c in core_copies:
+    for o, h, then, c in core_copies:
         c.wait_recv()
-        total = own[h, tgt] + crecv[h, o].astype(F32)
-        if o == 0:
-            acc1[h] = total
-        else:
-            send1[h, o - 1] = total.astype(BF)
-            dev = device(tgt, y, z, core) if h == 0 else device(x, tgt, z, core)
-            r = remote(
-                send1.at[h, o - 1], recv1.at[h, o - 1], s1s.at[h, o - 1], s1r.at[h, o - 1], dev
-            )
-            r.start()
-            copies1[h, o] = r
+        for first in ORDER:
+            tgt = (x + first) % 4 if h == 0 else (y + first) % 4
+            total = own[h, tgt, then] + crecv[h, o, tgt].astype(F32)
+            if first == 0:
+                acc1[h, o] = total
+            else:
+                send1[h, o, first - 1] = total.astype(BF)
+                dev = device(tgt, y, z, core) if h == 0 else device(x, tgt, z, core)
+                r = remote(
+                    send1.at[h, o, first - 1], recv1.at[h, o, first - 1],
+                    s1s.at[h, o, first - 1], s1r.at[h, o, first - 1], dev,
+                )
+                r.start()
+                copies1[h, o, first] = r
+
+    pl.semaphore_wait(heard.at[1], len(NEAR))
 
     z_small = [
         remote(
@@ -330,14 +323,14 @@
             r.start()
 
     copies2 = {}
-    for h in range(2):
-        for o in (1, 3, 2):
-            copies1[h, o].wait_recv()
-        for o in ORDER:
+    for o in ORDER:
+        for h in range(2):
+            for first in (1, 3, 2):
+                copies1[h, o, first].wait_recv()
             tgt = (y + o) % 4 if h == 0 else (x + o) % 4
-            total = acc1[h, tgt]
+            total = acc1[h, o]
             for k in range(3):
-                total = total + recv1[h, k, tgt].astype(F32)
+                total = total + recv1[h, o, k].astype(F32)
             if o == 0:
                 acc2[h] = total
             else:
@@ -451,8 +444,7 @@
             pltpu.VMEM((1, BINS, C1), BF),
             pltpu.VMEM((1, 512), jnp.int32),
             pltpu.VMEM((1, 512), jnp.int32),
-            pltpu.VMEM((STEP, C1), BF),
-            pltpu.VMEM((STEP, C1), BF),
+            pltpu.VMEM((2 * STEP, C1), BF),
             pltpu.VMEM((16, 1024), F32),
             pltpu.VMEM((KE * 4, BINS), F32),
             pltpu.VMEM((BINS, C0), F32),
@@ -467,8 +459,8 @@
             pltpu.VMEM((2, 4, 4, 16, C0), F32),
             pltpu.VMEM((2, 4, 4, 16, C0), BF),
             pltpu.VMEM((2, 4, 4, 16, C0), BF),
-            pltpu.VMEM((2, 3, 4, 16, C0), BF),
-            pltpu.VMEM((2, 3, 4, 16, C0), BF),
+            pltpu.VMEM((2, 4, 3, 16, C0), BF),
+            pltpu.VMEM((2, 4, 3, 16, C0), BF),
             pltpu.VMEM((2, 4, 16, C0), F32),
             pltpu.VMEM((2, 3, 16, C0), BF),
             pltpu.VMEM((2, 3, 16, C0), BF),
@@ -482,9 +474,10 @@
             pltpu.VMEM((16, 128), BF),
             pltpu.VMEM((4, 8, C0), F32),
             dma((7,)),
+            pltpu.SemaphoreType.REGULAR((2,)),
             dma((4,)), dma((4,)),
             dma((2, 4)), dma((2, 4)),
-            dma((2, 3)), dma((2, 3)),
+            dma((2, 4, 3)), dma((2, 4, 3)),
             dma((2, 3)), dma((2, 3)),
             dma((16,)), dma((16,)),
             dma((TILES,)), dma((32,)),

time: 52.6 us -> 48.9 us (0.930)
  Pallas kernels: 51.8 us -> 48 us
    pallas_call x1, Pallas kernels: 50.2 us -> 46.4 us  [local(): pl.pallas_call(kernel, out_shape=(jax.ShapeDtypeStruct((TILES, 16, 128),...]
where the time goes in v5:
time: 48.9 us; the launch traced here: 48.7 us
  Pallas kernels  48 us (98%)
  between operations  0.64 us (1%)
    pallas_call x1, Pallas kernels, local(): pl.pallas_call(kernel, out_shape=(jax.ShapeDtypeStruct((TILES, 16, 128),...  46.4 us
    pallas_call x1, Pallas kernels, local(): pl.pallas_call(finish, out_shape=(jax.ShapeDtypeStruct((KE * 4, C0), F32)...  1.6 us

profile of v5, /device:TPU:1, one launch (start us, length us, event | category | flops | bytes accessed | tf_op | source)
XLA Modules:
  0.0 48.7 jit_solution(2755543947336500259)
XLA Ops:
  0.6 46.4 %encoder_backward.1 = (bf16[24,16,128]{2,1,0:T(8,128)(2,1)}, f32[16,128]{1,0:T(8,128)}) custom-call(s32[1,512]{1,0:T(1,128)} %h_bases.1, bf16[60,768]{1,0:T(8,128)(2,1)} %h_embed.1, f32[768]{0:T(1024)} %h_bias.1, f32[768]{0:T(1024)} %h_gain.1, f32[3,768]{1,0:T(4,128)} %h_taps.1, bf16[768,896]{1,0:T(8,128)(2,1)} %h_widen.1, bf16[1,256,896]{2,1,0:T(8,128)(2,1)} %h_cot.1), custom_call_target="tpu_custom_call" | custom-call | tf_op jit(solution)/shard_map/encoder_backward/pallas_call | solution.py:429
  47.1 1.6 %finish.1 = (f32[60,768]{1,0:T(8,128)}, f32[768]{0:T(1024)}, f32[768]{0:T(1024)}, f32[3,768]{1,0:T(4,128)}, f32[14,96]{1,0:T(8,128)}) custom-call(bf16[24,16,128]{2,1,0:T(8,128)(2,1)} %get-tuple-element.12.agb, f32[16,128]{1,0:T(8,128)} %get-tuple-element.13.wid), custom_call_target="tpu_custom_call" | custom-call | tf_op jit(solution)/shard_map/finish/pallas_call | solution.py:492

commit v6 on v5

--- a/solution.py
+++ b/solution.py
@@ -17,7 +17,15 @@
 F32 = jnp.float32
 ORDER = (2, 1, 3, 0)
 PLANE = [(dc, dx, dy) for dx in (2, 1, 3, 0) for dy in (2, 1, 3, 0) for dc in (1, 0)][:-1]
-NEAR = (4, 12, 3, 13, 2, 14, 1, 15)
+NEAR = tuple(
+    [(0, 2, 0, 0), (0, 0, 2, 0), (0, 0, 0, 2), (0, 0, 0, 14), (1, 0, 0, 0)]
+    + [(0, k, 0, 0) for k in (1, 3)] + [(0, 0, k, 0) for k in (1, 3)] + [(0, 0, 0, k) for k in (1, 15)]
+)
+ROUNDS = (
+    NEAR[:-2],
+    ((0, 0, 0, 4), (0, 0, 0, 12), (1, 0, 0, 0)),
+    ((0, 0, 0, 4), (0, 0, 0, 12)),
+)
 GELU_A = 0.7978845608028654
 GELU_B = 0.044715
 
@@ -93,18 +101,38 @@
     def signal(sem, dev):
         pl.semaphore_signal(sem, inc=1, device_id=dev, device_id_type=MESH)
 
+    def near(dc, dx, dy, dz):
+        return device((x + dx) % 4, (y + dy) % 4, (z + dz) % 16, (core + dc) % 2)
+
     signal(barrier, right)
     signal(barrier, left)
-    for dz in NEAR:
-        signal(barrier, device(x, y, (z + dz) % 16, core))
-    for dc, dx, dy in PLANE:
-        signal(barrier, device((x + dx) % 4, (y + dy) % 4, z, (core + dc) % 2))
+    for step in NEAR:
+        signal(barrier, near(*step))
 
     def remote(src, dst, send, recv, dev):
         return pltpu.make_async_remote_copy(
             src_ref=src, dst_ref=dst, send_sem=send, recv_sem=recv,
             device_id=dev, device_id_type=MESH,
         )
+
+    pl.semaphore_wait(barrier, 2 + len(NEAR))
+
+    halo = [
+        remote(h_bases, lb, hs.at[0], hr.at[0], right),
+        remote(h_bases, rb, hs.at[1], hr.at[1], left),
+        remote(h_cot.at[0, pl.ds(BINS - STEP, STEP)], rim.at[pl.ds(0, STEP)], hs.at[2], hr.at[2], right),
+        remote(h_cot.at[0, pl.ds(0, STEP)], rim.at[pl.ds(STEP, STEP)], hs.at[3], hr.at[3], left),
+    ]
+    for c in halo:
+        c.start()
+
+    def pass_on(k):
+        if k > 0:
+            pl.semaphore_wait(heard.at[k - 1], len(ROUNDS[k - 1]))
+        for step in ROUNDS[k]:
+            signal(heard.at[k], near(*step))
+
+    pass_on(0)
 
     p, col = iota((C0, BINS), 0), iota((C0, BINS), 1)
     tap_of, base_of = iota((KE * 4, 16), 0) >> 2, (iota((KE * 4, BINS), 0) & 3).astype(F32)
@@ -162,26 +190,13 @@
     emb[...] = dot(paired[...].astype(BF), w_embed[...], 0, 0)
 
     def own_forward(i, _):
-        for k in range(2):
-            at = aligned(i * 32 + 16 * k)
+        for k in range(4):
+            at = aligned(i * 64 + 16 * k)
             forward(at, aligned(at + STEP), None)
         return 0
 
-    lax.fori_loop(0, BINS // 32, own_forward, 0)
+    lax.fori_loop(0, BINS // 64, own_forward, 0)
     loads[5].wait()
-
-    pl.semaphore_wait(barrier, 2 + len(NEAR) + len(PLANE))
-
-    halo = [
-        remote(bases, lb, hs.at[0], hr.at[0], right),
-        remote(bases, rb, hs.at[1], hr.at[1], left),
-        remote(cot.at[0, pl.ds(BINS - STEP, STEP)], rim.at[pl.ds(0, STEP)], hs.at[2], hr.at[2], right),
-        remote(cot.at[0, pl.ds(0, STEP)], rim.at[pl.ds(STEP, STEP)], hs.at[3], hr.at[3], left),
-    ]
-    for c in halo:
-        c.start()
-    for dz in NEAR:
-        signal(heard.at[0], device(x, y, (z + dz) % 16, core))
 
     loads[6].wait()
     dblk[STEP : STEP + BINS] = dot(cot[0], w_widen[...], 1, 1).astype(BF)
@@ -199,17 +214,11 @@
                 total = total + new[k]
             totals[k] = total
 
-    def inner(i, _):
-        mix(5 + 2 * i)
-        mix(6 + 2 * i)
-        add_up([backward(5 + 2 * i), backward(6 + 2 * i)])
-        return 0
-
-    lax.fori_loop(0, 3, inner, 0)
-
-    pl.semaphore_wait(heard.at[0], len(NEAR))
-    for dz in NEAR:
-        signal(heard.at[1], device(x, y, (z + dz) % 16, core))
+    for i in range(5, 11):
+        mix(i)
+    add_up([backward(i) for i in range(5, 11)])
+
+    pass_on(1)
 
     halo[0].wait_recv()
     halo[1].wait_recv()
@@ -250,6 +259,8 @@
     for c in range(TILES):
         i, j = c // 6, c % 6
         smb[c] = sm[16 * i : 16 * i + 16, 128 * j : 128 * j + 128].astype(BF)
+
+    pass_on(2)
 
     rs_copies = []
     for k in range(TILES):
@@ -298,8 +309,6 @@
                 )
                 r.start()
                 copies1[h, o, first] = r
-
-    pl.semaphore_wait(heard.at[1], len(NEAR))
 
     z_small = [
         remote(
@@ -342,6 +351,8 @@
                 )
                 r.start()
                 copies2[h, o] = r
+
+    pl.semaphore_wait(heard.at[2], len(ROUNDS[2]))
 
     zcopies = []
     for h in range(2):
@@ -474,7 +485,7 @@
             pltpu.VMEM((16, 128), BF),
             pltpu.VMEM((4, 8, C0), F32),
             dma((7,)),
-            pltpu.SemaphoreType.REGULAR((2,)),
+            pltpu.SemaphoreType.REGULAR((3,)),
             dma((4,)), dma((4,)),
             dma((2, 4)), dma((2, 4)),
             dma((2, 4, 3)), dma((2, 4, 3)),

time: 48.9 us -> 48.7 us (level)
  no operation moved by 1% of the time
where the time goes in v6:
time: 48.7 us; the launch traced here: 48.5 us
  Pallas kernels  47.9 us (98%)
  between operations  0.64 us (1%)
    pallas_call x1, Pallas kernels, local(): pl.pallas_call(kernel, out_shape=(jax.ShapeDtypeStruct((TILES, 16, 128),...  46.3 us
    pallas_call x1, Pallas kernels, local(): pl.pallas_call(finish, out_shape=(jax.ShapeDtypeStruct((KE * 4, C0), F32)...  1.6 us

profile of v6, /device:TPU:1, one launch (start us, length us, event | category | flops | bytes accessed | tf_op | source)
XLA Modules:
  0.0 48.5 jit_solution(16261820617470106119)
XLA Ops:
  0.6 46.3 %encoder_backward.1 = (bf16[24,16,128]{2,1,0:T(8,128)(2,1)}, f32[16,128]{1,0:T(8,128)}) custom-call(s32[1,512]{1,0:T(1,128)} %h_bases.1, bf16[60,768]{1,0:T(8,128)(2,1)} %h_embed.1, f32[768]{0:T(1024)} %h_bias.1, f32[768]{0:T(1024)} %h_gain.1, f32[3,768]{1,0:T(4,128)} %h_taps.1, bf16[768,896]{1,0:T(8,128)(2,1)} %h_widen.1, bf16[1,256,896]{2,1,0:T(8,128)(2,1)} %h_cot.1), custom_call_target="tpu_custom_call" | custom-call | tf_op jit(solution)/shard_map/encoder_backward/pallas_call | solution.py:440
  46.9 1.6 %finish.1 = (f32[60,768]{1,0:T(8,128)}, f32[768]{0:T(1024)}, f32[768]{0:T(1024)}, f32[3,768]{1,0:T(4,128)}, f32[14,96]{1,0:T(8,128)}) custom-call(bf16[24,16,128]{2,1,0:T(8,128)(2,1)} %get-tuple-element.12.agb, f32[16,128]{1,0:T(8,128)} %get-tuple-element.13.wid), custom_call_target="tpu_custom_call" | custom-call | tf_op jit(solution)/shard_map/finish/pallas_call | solution.py:503

commit v7 on v6

--- a/solution.py
+++ b/solution.py
@@ -21,11 +21,8 @@
     [(0, 2, 0, 0), (0, 0, 2, 0), (0, 0, 0, 2), (0, 0, 0, 14), (1, 0, 0, 0)]
     + [(0, k, 0, 0) for k in (1, 3)] + [(0, 0, k, 0) for k in (1, 3)] + [(0, 0, 0, k) for k in (1, 15)]
 )
-ROUNDS = (
-    NEAR[:-2],
-    ((0, 0, 0, 4), (0, 0, 0, 12), (1, 0, 0, 0)),
-    ((0, 0, 0, 4), (0, 0, 0, 12)),
-)
+ALONG = ((0, 0, 0, 4), (0, 0, 0, 12))
+ROUNDS = (NEAR[:-2], ((1, 0, 0, 0),), ALONG, ALONG)
 GELU_A = 0.7978845608028654
 GELU_B = 0.044715
 
@@ -126,13 +123,14 @@
     for c in halo:
         c.start()
 
-    def pass_on(k):
-        if k > 0:
-            pl.semaphore_wait(heard.at[k - 1], len(ROUNDS[k - 1]))
+    def tell(k):
         for step in ROUNDS[k]:
             signal(heard.at[k], near(*step))
 
-    pass_on(0)
+    def hear(k):
+        pl.semaphore_wait(heard.at[k], len(ROUNDS[k]))
+
+    tell(0)
 
     p, col = iota((C0, BINS), 0), iota((C0, BINS), 1)
     tap_of, base_of = iota((KE * 4, 16), 0) >> 2, (iota((KE * 4, BINS), 0) & 3).astype(F32)
@@ -196,6 +194,9 @@
         return 0
 
     lax.fori_loop(0, BINS // 64, own_forward, 0)
+    hear(0)
+    tell(1)
+    tell(2)
     loads[5].wait()
 
     loads[6].wait()
@@ -217,8 +218,6 @@
     for i in range(5, 11):
         mix(i)
     add_up([backward(i) for i in range(5, 11)])
-
-    pass_on(1)
 
     halo[0].wait_recv()
     halo[1].wait_recv()
@@ -260,7 +259,7 @@
         i, j = c // 6, c % 6
         smb[c] = sm[16 * i : 16 * i + 16, 128 * j : 128 * j + 128].astype(BF)
 
-    pass_on(2)
+    hear(1)
 
     rs_copies = []
     for k in range(TILES):
@@ -291,6 +290,9 @@
             core_copies.append((o, h, then, c))
     for h in range(2):
         own[h] = dot(cot_t[0, h], block[...], 1, 0).reshape(4, 4, 16, C0)
+
+    hear(2)
+    tell(3)
 
     copies1 = {}
     for o, h, then, c in core_copies:
@@ -352,7 +354,7 @@
                 r.start()
                 copies2[h, o] = r
 
-    pl.semaphore_wait(heard.at[2], len(ROUNDS[2]))
+    hear(3)
 
     zcopies = []
     for h in range(2):
@@ -485,7 +487,7 @@
             pltpu.VMEM((16, 128), BF),
             pltpu.VMEM((4, 8, C0), F32),
             dma((7,)),
-            pltpu.SemaphoreType.REGULAR((3,)),
+            pltpu.SemaphoreType.REGULAR((4,)),
             dma((4,)), dma((4,)),
             dma((2, 4)), dma((2, 4)),
             dma((2, 4, 3)), dma((2, 4, 3)),

time: 48.7 us -> 48.8 us (level)
  no operation moved by 1% of the time
where the time goes in v7:
time: 48.8 us; the launch traced here: 48.7 us
  Pallas kernels  48 us (98%)
  between operations  0.64 us (1%)
    pallas_call x1, Pallas kernels, local(): pl.pallas_call(kernel, out_shape=(jax.ShapeDtypeStruct((TILES, 16, 128),...  46.4 us
    pallas_call x1, Pallas kernels, local(): pl.pallas_call(finish, out_shape=(jax.ShapeDtypeStruct((KE * 4, C0), F32)...  1.6 us

profile of v7, /device:TPU:1, one launch (start us, length us, event | category | flops | bytes accessed | tf_op | source)
XLA Modules:
  0.0 48.7 jit_solution(9859654957923723713)
XLA Ops:
  0.6 46.4 %encoder_backward.1 = (bf16[24,16,128]{2,1,0:T(8,128)(2,1)}, f32[16,128]{1,0:T(8,128)}) custom-call(s32[1,512]{1,0:T(1,128)} %h_bases.1, bf16[60,768]{1,0:T(8,128)(2,1)} %h_embed.1, f32[768]{0:T(1024)} %h_bias.1, f32[768]{0:T(1024)} %h_gain.1, f32[3,768]{1,0:T(4,128)} %h_taps.1, bf16[768,896]{1,0:T(8,128)(2,1)} %h_widen.1, bf16[1,256,896]{2,1,0:T(8,128)(2,1)} %h_cot.1), custom_call_target="tpu_custom_call" | custom-call | tf_op jit(solution)/shard_map/encoder_backward/pallas_call | solution.py:442
  47.1 1.6 %finish.1 = (f32[60,768]{1,0:T(8,128)}, f32[768]{0:T(1024)}, f32[768]{0:T(1024)}, f32[3,768]{1,0:T(4,128)}, f32[14,96]{1,0:T(8,128)}) custom-call(bf16[24,16,128]{2,1,0:T(8,128)(2,1)} %get-tuple-element.12.agb, f32[16,128]{1,0:T(8,128)} %get-tuple-element.13.wid), custom_call_target="tpu_custom_call" | custom-call | tf_op jit(solution)/shard_map/finish/pallas_call | solution.py:505
